TPU v7x, 32 devices: a whole 2x2x4 slice. The times are simulated.
32 devices in a mesh: groups: 2 (over y), dom: 8 (over z, x), edge: 2 (over core).
Axes of the slice: x: 2, y: 2, z: 4, core: 2. Of those that a mesh axis runs over, the one named last changes fastest.
Arguments:
- entities: float32 [400, 4096], P(None, ('groups', 'dom')), parts along dimension 1, may hold values from -2.5 to 2.5
- entity_state: float32 [4096], P(('groups', 'dom')), parts along dimension 0, may hold values from 0.1 to 1
- relations: float32 [400, 4096], P(None, 'groups'), parts along dimension 1, may hold values from -4 to 4
- relation_state: float32 [4096], P('groups'), parts along dimension 0, may hold values from 0.1 to 1
- src_rows: int32 [6, 128, 128], P(None, ('groups', 'dom', 'edge')), parts along dimension 1, may hold values from 0 to 255
- rel_ids: int32 [6, 128, 128], P(None, ('groups', 'dom', 'edge')), parts along dimension 1, may hold values from 0 to 2047
- dst_rows: int32 [6, 128, 128], P(None, ('groups', 'dom', 'edge')), parts along dimension 1, may hold values from 0 to 255
- counts: int32 [6, 128], P(None, ('groups', 'dom', 'edge')), parts along dimension 1, may hold values from 1 to 128
- neg_blocks: int32 [6, 128], P(None, ('groups', 'dom', 'edge')), parts along dimension 1, may hold values from 0 to 3
Outputs:
- new_entities: float32 [400, 4096], P(None, ('groups', 'dom')), parts along dimension 1
- new_entity_state: float32 [4096], P(('groups', 'dom')), parts along dimension 0
- new_relations: float32 [400, 4096], P(None, 'groups'), parts along dimension 1
- new_relation_state: float32 [4096], P('groups'), parts along dimension 0
There are 2 independent parts, one for each index of `groups`. A program takes and returns all parts, laid end to end along the dimension named above; each array names one. Nothing has to cross between parts.
All inputs are finite; a program needn't handle non-finite values.
Results may differ from a plain program's by a relative error of at most 0.0024.
Values may be sent and summed in bfloat16 or wider, within the bound.
No kernel may reach another device: no remote copies, remote signals or barrier semaphores. Data moves between devices by JAX's collectives and lax.ppermute only.
A program may use at most 128 MiB of HBM per device.

v0:
```python
import jax
import jax.numpy as jnp
from jax import lax
from jax.sharding import PartitionSpec as P

learn_rate = 0.1


def passed_along(shard, axis, by):
    devices = lax.axis_size(axis)
    return lax.ppermute(shard, axis, [(i, (i + by) % devices) for i in range(devices)])


def block_terms(
    src_table, dst_table, rel_table, src_idx, rel_idx, dst_idx, valid_count, negative, rel_total
):
    half_dim = src_table.shape[0] // 2
    source_lo = src_table[:, src_idx]
    target_lo = dst_table[:, dst_idx]
    source = source_lo.astype(jnp.float32)
    relvec = rel_table[:, rel_idx].astype(jnp.float32)
    query_re = source[:half_dim] * relvec[:half_dim] - source[half_dim:] * relvec[half_dim:]
    query_im = source[:half_dim] * relvec[half_dim:] + source[half_dim:] * relvec[:half_dim]
    query_lo = jnp.concatenate([query_re, query_im], axis=0).astype(jnp.bfloat16)
    slots = jnp.arange(src_idx.shape[1], dtype=jnp.int32)
    valid = (slots[None, :] < valid_count[:, None]).astype(jnp.float32)
    neg_valid = valid[negative]
    neg_lo = target_lo[:, negative, :]
    positive = jnp.einsum("dbi,dbi->bi", query_lo, target_lo, preferred_element_type=jnp.float32)
    scores = jnp.einsum("dbi,dbj->bij", query_lo, neg_lo, preferred_element_type=jnp.float32)
    grad_pos = -jax.nn.sigmoid(-positive) * valid
    weight = (
        jax.nn.sigmoid(scores) * valid[:, :, None] * neg_valid[:, None, :] / src_idx.shape[1]
    ).astype(jnp.bfloat16)
    dquery = grad_pos[None] * target_lo + jnp.einsum(
        "bij,dbj->dbi", weight, neg_lo, preferred_element_type=jnp.float32
    )
    dpos = grad_pos[None] * query_lo
    dneg = jnp.einsum("bij,dbi->dbj", weight, query_lo, preferred_element_type=jnp.float32)
    dq_re, dq_im = (dquery[:half_dim], dquery[half_dim:])
    dsource = jnp.concatenate(
        [
            dq_re * relvec[:half_dim] + dq_im * relvec[half_dim:],
            dq_im * relvec[:half_dim] - dq_re * relvec[half_dim:],
        ],
        axis=0,
    )
    drelation = jnp.concatenate(
        [
            dq_re * source[:half_dim] + dq_im * source[half_dim:],
            dq_im * source[:half_dim] - dq_re * source[half_dim:],
        ],
        axis=0,
    )
    width = src_table.shape[0]
    rows = src_table.shape[1]
    grad_src = (
        jnp.zeros((width, rows), jnp.float32)
        .at[:, src_idx.reshape(-1)]
        .add(dsource.reshape(width, -1))
    )
    grad_dst = (
        jnp.zeros((width, rows), jnp.float32)
        .at[:, dst_idx.reshape(-1)]
        .add(dpos.reshape(width, -1))
    )
    grad_dst = grad_dst.at[:, dst_idx[negative].reshape(-1)].add(dneg.reshape(width, -1))
    rel_total = rel_total.at[:, rel_idx.reshape(-1)].add(drelation.reshape(width, -1))
    return (grad_src, grad_dst, rel_total)


def adagrad(table, state, grad):
    state = state + jnp.mean(grad * grad, axis=0)
    return (table - learn_rate * grad / jnp.sqrt(state)[None, :], state)


def on_device(
    entities,
    entity_state,
    relations,
    relation_state,
    src_rows,
    rel_ids,
    dst_rows,
    counts,
    neg_blocks,
):
    rounds = src_rows.shape[0]
    rel16 = relations.astype(jnp.bfloat16)
    rel_grad = jnp.zeros(relations.shape, jnp.float32)
    embedding = entities
    state = entity_state
    for round_index in range(rounds):
        table16 = embedding.astype(jnp.bfloat16)
        if round_index == 0:
            dest16 = table16
        else:
            dest16 = passed_along(table16, "dom", -round_index)
        grad_src, grad_dst, rel_grad = block_terms(
            table16,
            dest16,
            rel16,
            src_rows[round_index],
            rel_ids[round_index],
            dst_rows[round_index],
            counts[round_index],
            neg_blocks[round_index],
            rel_grad,
        )
        if round_index == 0:
            returned = grad_dst
        else:
            returned = passed_along(grad_dst, "dom", round_index)
        total = lax.psum(grad_src + returned, "edge")
        embedding, state = adagrad(embedding, state, total)
    total_rel = lax.psum(rel_grad, ("dom", "edge"))
    rel_new, rel_state = adagrad(relations, relation_state, total_rel)
    return (embedding, state, rel_new, rel_state)


def solution(mesh):
    return jax.shard_map(
        on_device,
        mesh=mesh,
        in_specs=(
            P(None, ("groups", "dom")),
            P(("groups", "dom")),
            P(None, "groups"),
            P("groups"),
            P(None, ("groups", "dom", "edge"), None),
            P(None, ("groups", "dom", "edge"), None),
            P(None, ("groups", "dom", "edge"), None),
            P(None, ("groups", "dom", "edge")),
            P(None, ("groups", "dom", "edge")),
        ),
        out_specs=(
            P(None, ("groups", "dom")),
            P(("groups", "dom")),
            P(None, "groups"),
            P("groups"),
        ),
        check_vma=False,
    )
```

profile of v0, /device:TPU:0, one launch (start us, length us, event | category | flops | bytes accessed | tf_op | source)
XLA Modules:
  0.0 666.7 jit_solution(5807443774522489409)
XLA Ops:
  12.7 5.0 copy.118
  17.7 2.5 convert_element_type.173
  21.1 2.6 gather_fusion.2
  26.5 2.6 gather_fusion.1
  33.0 2.6 gather_fusion
  52.1 2.5 copy.124
  55.6 2.5 copy.127
  60.8 2.5 copy.129
  63.2 5.2 scatter_custom_fusion
  68.5 4.4 scatter_custom_fusion.1
  73.2 4.5 scatter_fusion
  109.6 6.4 collective-permute-start
  116.0 2.8 gather_fusion.6
  123.6 2.6 gather_fusion.8
  136.5 4.4 scatter_custom_fusion.3
  140.9 4.5 scatter_fusion.1
  146.9 2.5 multiply_add_fusion.4
  150.4 2.5 copy.143
  152.9 8.6 %collective-permute-done.1 = f32[400,256]{0,1:T(8,128)S(1)} collective-permute-done((f32[400,256]{0,1:T(8,128)S(1)}, f32[400,256]{0,1:T(8,128)S(1)}, u32[]{:S(2)}, u32[]{:S(2)}) %collective-permute-start.1) | collective-permute-done | bytes 409632 | tf_op jit(solution)/shard_map/ppermute | solution.py:11
  161.5 4.6 scatter_fusion.2
  173.9 9.2 %all-reduce.10.cloned.1.call-done = f32[400,256]{0,1:T(8,128)} async-done(((f32[400,256]{0,1:T(8,128)}), f32[400,256]{0,1:T(8,128)}) %all-reduce.10.cloned.1.call-update) | async-done | bytes 409616 | tf_op jit(solution)/shard_map/psum | solution.py:114
  187.8 3.6 collective-permute-start.2
  197.4 2.8 gather_fusion.14
  210.4 4.4 scatter_custom_fusion.6
  214.8 4.7 scatter_fusion.3
  221.7 2.5 multiply_add_fusion.3
  225.2 2.5 copy.156
  227.6 7.8 %collective-permute-done.3 = f32[400,256]{0,1:T(8,128)S(1)} collective-permute-done((f32[400,256]{0,1:T(8,128)S(1)}, f32[400,256]{0,1:T(8,128)S(1)}, u32[]{:S(2)}, u32[]{:S(2)}) %collective-permute-start.3) | collective-permute-done | bytes 409632 | tf_op jit(solution)/shard_map/ppermute | solution.py:11
  235.4 4.5 scatter_fusion.4
  247.2 11.8 %all-reduce.12.cloned.1.call-done = f32[400,256]{0,1:T(8,128)} async-done(((f32[400,256]{0,1:T(8,128)}), f32[400,256]{0,1:T(8,128)}) %all-reduce.12.cloned.1.call-update) | async-done | bytes 409616 | tf_op jit(solution)/shard_map/psum | solution.py:114
  262.5 4.0 collective-permute-start.4
  266.6 2.6 gather_fusion.18
  274.0 2.6 gather_fusion.20
  288.0 4.4 scatter_custom_fusion.9
  292.4 4.5 scatter_fusion.5
  300.5 2.5 multiply_add_fusion.2
  306.5 17.4 %collective-permute-done.5 = f32[400,256]{0,1:T(8,128)S(1)} collective-permute-done((f32[400,256]{0,1:T(8,128)S(1)}, f32[400,256]{0,1:T(8,128)S(1)}, u32[]{:S(2)}, u32[]{:S(2)}) %collective-permute-start.5) | collective-permute-done | bytes 409632 | tf_op jit(solution)/shard_map/ppermute | solution.py:11
  323.8 4.6 scatter_fusion.6
  336.3 11.8 %all-reduce.14.cloned.1.call-done = f32[400,256]{0,1:T(8,128)} async-done(((f32[400,256]{0,1:T(8,128)}), f32[400,256]{0,1:T(8,128)}) %all-reduce.14.cloned.1.call-update) | async-done | bytes 409616 | tf_op jit(solution)/shard_map/psum | solution.py:114
  352.3 2.7 collective-permute-start.6
  355.0 2.6 gather_fusion.24
  362.4 4.9 collective-permute-done.6
  367.3 2.6 gather_fusion.26
  380.2 4.4 scatter_custom_fusion.12
  384.5 4.7 scatter_fusion.7
  390.8 2.5 multiply_add_fusion.1
  396.8 18.0 %collective-permute-done.7 = f32[400,256]{0,1:T(8,128)S(1)} collective-permute-done((f32[400,256]{0,1:T(8,128)S(1)}, f32[400,256]{0,1:T(8,128)S(1)}, u32[]{:S(2)}, u32[]{:S(2)}) %collective-permute-start.7) | collective-permute-done | bytes 409632 | tf_op jit(solution)/shard_map/ppermute | solution.py:11
  414.8 4.5 scatter_fusion.8
  423.5 6.3 scatter_custom_fusion.18
  430.5 7.8 %scatter_fusion.11 = f32[400,2048]{0,1:T(8,128)} fusion(f32[400,2048]{0,1:T(8,128)} %scatter_custom_fusion.18, s32[512]{0:T(512)S(1)} %bitcast.594, f32[512,400]{1,0:T(8,128)S(1)} %copy.199), kind=kCustom, calls=%fused_computation.55 | custom fusion | flops 204800 | bytes 2459648 | tf_op jit(solution)/shard_map/scatter-add | solution.py:68
  446.1 10.2 %collective-permute-done.8 = bf16[400,256]{0,1:T(8,128)(2,1)S(1)} collective-permute-done((bf16[400,256]{0,1:T(8,128)(2,1)S(1)}, bf16[400,256]{0,1:T(8,128)(2,1)S(1)}, u32[]{:S(2)}, u32[]{:S(2)}) %collective-permute-start.8) | collective-permute-done | bytes 204832 | tf_op jit(solution)/shard_map/ppermute | solution.py:11
  456.3 2.6 gather_fusion.32
  466.3 4.4 scatter_custom_fusion.15
  470.7 4.6 scatter_fusion.9
  478.2 11.0 %collective-permute-done.9 = f32[400,256]{0,1:T(8,128)S(1)} collective-permute-done((f32[400,256]{0,1:T(8,128)S(1)}, f32[400,256]{0,1:T(8,128)S(1)}, u32[]{:S(2)}, u32[]{:S(2)}) %collective-permute-start.9) | collective-permute-done | bytes 409632 | tf_op jit(solution)/shard_map/ppermute | solution.py:11
  489.3 3.8 scatter_fusion.10
  494.5 7.8 %scatter_fusion.12 = f32[400,2048]{0,1:T(8,128)} fusion(f32[400,2048]{0,1:T(8,128)} %scatter_fusion.11, s32[512]{0:T(512)S(1)} %bitcast.591, f32[512,400]{1,0:T(8,128)S(1)} %copy.201), kind=kCustom, calls=%fused_computation.56 | custom fusion | flops 204800 | bytes 2459648 | tf_op jit(solution)/shard_map/scatter-add | solution.py:68
  502.8 8.0 %scatter_fusion.13 = f32[400,2048]{0,1:T(8,128)} fusion(f32[400,2048]{0,1:T(8,128)} %scatter_fusion.12, s32[512]{0:T(512)S(1)} %bitcast.590, f32[512,400]{1,0:T(8,128)S(1)} %copy.203), kind=kCustom, calls=%fused_computation.57 | custom fusion | flops 204800 | bytes 2459648 | tf_op jit(solution)/shard_map/scatter-add | solution.py:68
  511.3 7.8 %scatter_fusion.14 = f32[400,2048]{0,1:T(8,128)} fusion(f32[400,2048]{0,1:T(8,128)} %scatter_fusion.13, s32[512]{0:T(512)S(1)} %bitcast.589, f32[512,400]{1,0:T(8,128)S(1)} %copy.205), kind=kCustom, calls=%fused_computation.58 | custom fusion | flops 204800 | bytes 2459648 | tf_op jit(solution)/shard_map/scatter-add | solution.py:68
  519.6 7.8 %scatter_fusion.15 = f32[400,2048]{0,1:T(8,128)} fusion(f32[400,2048]{0,1:T(8,128)} %scatter_fusion.14, s32[512]{0:T(512)S(1)} %bitcast.588, f32[512,400]{1,0:T(8,128)S(1)} %copy.207), kind=kCustom, calls=%fused_computation.59 | custom fusion | flops 204800 | bytes 2459648 | tf_op jit(solution)/shard_map/scatter-add | solution.py:68
  531.4 114.7 %all-reduce.20.cloned.1.call-done = f32[400,2048]{0,1:T(8,128)} async-done(((f32[400,2048]{0,1:T(8,128)}), f32[400,2048]{0,1:T(8,128)}) %all-reduce.20.cloned.1.call-update) | async-done | bytes 3276816 | tf_op jit(solution)/shard_map/psum | solution.py:116
  646.1 2.7 multiply_reduce_fusion
  649.6 4.9 divide_subtract_fusion
  654.5 5.2 copy.210
  (560 shorter events, 209.5 us)
Async XLA Ops:
  7.2 98.2 %all-reduce.8.cloned.1.call-start = ((), (), s32[]{:S(2)}) async-start(), calls=%async_computation | async-start | bytes 1048576 | tf_op jit(solution)/shard_map/psum | solution.py:114
  21.1 86.8 %copy-start.6 = (f32[400,256]{0,1:T(8,128)}, f32[400,256]{0,1:T(8,128)S(1)}, u32[]{:S(2)}) copy-start(f32[400,256]{0,1:T(8,128)S(1)} %copy.130) | copy-start | bytes 1228804
  25.9 16.2 %copy-start.120 = (s32[4]{0:T(128)}, s32[4]{0:T(128)S(1)}, u32[]{:S(2)}) copy-start(s32[4]{0:T(128)S(1)} %get-tuple-element.25) | copy-start | bytes 52
  72.9 12.0 %copy-start.111 = (s32[512]{0:T(512)S(1)}, s32[512]{0:T(512)}, u32[]{:S(2)}) copy-start(s32[512]{0:T(512)} %get-tuple-element.121) | copy-start | bytes 6148
  73.0 12.6 %copy-start.109 = (s32[512]{0:T(512)S(1)}, s32[512]{0:T(512)}, u32[]{:S(2)}) copy-start(s32[512]{0:T(512)} %get-tuple-element.115) | copy-start | bytes 6148
  73.0 13.1 %copy-start.146 = (s32[4]{0:T(128)S(1)}, s32[4]{0:T(128)}, u32[]{:S(2)}) copy-start(s32[4]{0:T(128)} %get-tuple-element.17) | copy-start | bytes 52
  73.0 13.1 %copy-start.147 = (s32[4]{0:T(128)S(1)}, s32[4]{0:T(128)}, u32[]{:S(2)}) copy-start(s32[4]{0:T(128)} %get-tuple-element.18) | copy-start | bytes 52
  73.0 13.2 %copy-start.66 = (s32[4,128]{1,0:T(4,128)S(1)}, s32[4,128]{1,0:T(4,128)}, u32[]{:S(2)}) copy-start(s32[4,128]{1,0:T(4,128)} %get-tuple-element.103) | copy-start | bytes 6148
  73.0 14.2 %copy-start.126 = (s32[1,4,128]{2,1,0:T(4,128)S(1)}, s32[1,4,128]{2,1,0:T(4,128)}, u32[]{:S(2)}) copy-start(s32[1,4,128]{2,1,0:T(4,128)} %get-tuple-element.96) | copy-start | bytes 6148
  73.0 14.8 %copy-start.65 = (s32[4,128]{1,0:T(4,128)S(1)}, s32[4,128]{1,0:T(4,128)}, u32[]{:S(2)}) copy-start(s32[4,128]{1,0:T(4,128)} %get-tuple-element.104) | copy-start | bytes 6148
  73.0 15.9 %copy-start.125 = (s32[1,4,128]{2,1,0:T(4,128)S(1)}, s32[1,4,128]{2,1,0:T(4,128)}, u32[]{:S(2)}) copy-start(s32[1,4,128]{2,1,0:T(4,128)} %get-tuple-element.95) | copy-start | bytes 6148
  73.0 16.5 %copy-start.123 = (s32[1,4,128]{2,1,0:T(4,128)S(1)}, s32[1,4,128]{2,1,0:T(4,128)}, u32[]{:S(2)}) copy-start(s32[1,4,128]{2,1,0:T(4,128)} %get-tuple-element.111) | copy-start | bytes 6148
  73.0 17.0 %copy-start.144 = (s32[4]{0:T(128)S(1)}, s32[4]{0:T(128)}, u32[]{:S(2)}) copy-start(s32[4]{0:T(128)} %get-tuple-element.16) | copy-start | bytes 52
  73.0 17.0 %copy-start.145 = (s32[4]{0:T(128)S(1)}, s32[4]{0:T(128)}, u32[]{:S(2)}) copy-start(s32[4]{0:T(128)} %get-tuple-element.21) | copy-start | bytes 52
  73.1 17.0 %copy-start.64 = (s32[4,128]{1,0:T(4,128)S(1)}, s32[4,128]{1,0:T(4,128)}, u32[]{:S(2)}) copy-start(s32[4,128]{1,0:T(4,128)} %get-tuple-element.105) | copy-start | bytes 6148
  73.1 18.2 %copy-start.124 = (s32[1,4,128]{2,1,0:T(4,128)S(1)}, s32[1,4,128]{2,1,0:T(4,128)}, u32[]{:S(2)}) copy-start(s32[1,4,128]{2,1,0:T(4,128)} %get-tuple-element.99) | copy-start | bytes 6148
  73.1 18.8 %copy-start.62 = (s32[4,128]{1,0:T(4,128)S(1)}, s32[4,128]{1,0:T(4,128)}, u32[]{:S(2)}) copy-start(s32[4,128]{1,0:T(4,128)} %get-tuple-element.100) | copy-start | bytes 6148
  73.1 20.0 %copy-start.122 = (s32[1,4,128]{2,1,0:T(4,128)S(1)}, s32[1,4,128]{2,1,0:T(4,128)}, u32[]{:S(2)}) copy-start(s32[1,4,128]{2,1,0:T(4,128)} %get-tuple-element.94) | copy-start | bytes 6148
  73.1 24.0 %copy-start.117 = (s32[4]{0:T(128)S(1)}, s32[4]{0:T(128)}, u32[]{:S(2)}) copy-start(s32[4]{0:T(128)} %get-tuple-element.23) | copy-start | bytes 52
  73.1 24.0 %copy-start.118 = (s32[4]{0:T(128)S(1)}, s32[4]{0:T(128)}, u32[]{:S(2)}) copy-start(s32[4]{0:T(128)} %get-tuple-element.24) | copy-start | bytes 52
  73.1 24.7 %copy-start.113 = (s32[4]{0:T(128)S(1)}, s32[4]{0:T(128)}, u32[]{:S(2)}) copy-start(s32[4]{0:T(128)} %get-tuple-element.22) | copy-start | bytes 52
  73.1 24.7 %copy-start.115 = (s32[4]{0:T(128)S(1)}, s32[4]{0:T(128)}, u32[]{:S(2)}) copy-start(s32[4]{0:T(128)} %get-tuple-element.27) | copy-start | bytes 52
  73.1 25.3 %copy-start.108 = (s32[512]{0:T(512)S(1)}, s32[512]{0:T(512)}, u32[]{:S(2)}) copy-start(s32[512]{0:T(512)} %get-tuple-element.122) | copy-start | bytes 6148
  73.1 25.9 %copy-start.75 = (s32[1024]{0:T(1024)S(1)}, s32[1024]{0:T(1024)}, u32[]{:S(2)}) copy-start(s32[1024]{0:T(1024)} %get-tuple-element.134) | copy-start | bytes 12292
  79.6 103.6 %all-reduce.10.cloned.1.call-start = ((), (), s32[]{:S(2)}) async-start(), calls=%async_computation.1 | async-start | bytes 1048576 | tf_op jit(solution)/shard_map/psum | solution.py:114
  82.6 16.5 %copy-start.139 = (s32[1024]{0:T(1024)}, s32[1024]{0:T(1024)S(1)}, u32[]{:S(2)}) copy-start(s32[1024]{0:T(1024)S(1)} %pad_clamp_fusion.16) | copy-start | bytes 12292
  86.1 13.0 %copy-start.138 = (s32[1024]{0:T(1024)}, s32[1024]{0:T(1024)S(1)}, u32[]{:S(2)}) copy-start(s32[1024]{0:T(1024)S(1)} %pad_clamp_fusion.12) | copy-start | bytes 12292
  109.6 12.2 %copy-start.10 = (f32[400,4,128]{2,0,1:T(8,128)S(1)}, f32[400,4,128]{2,0,1:T(8,128)}, u32[]{:S(2)}) copy-start(f32[400,4,128]{2,0,1:T(8,128)} %bitcast_bitcast_fusion.26) | copy-start | bytes 2457604
  109.6 14.0 %copy-start.86 = (s32[1024]{0:T(1024)S(1)}, s32[1024]{0:T(1024)}, u32[]{:S(2)}) copy-start(s32[1024]{0:T(1024)} %pad_clamp_fusion.17) | copy-start | bytes 12292
  109.6 14.0 %collective-permute-start = (bf16[400,256]{0,1:T(8,128)(2,1)S(1)}, bf16[400,256]{0,1:T(8,128)(2,1)S(1)}, u32[]{:S(2)}, u32[]{:S(2)}) collective-permute-start(bf16[400,256]{0,1:T(8,128)(2,1)S(1)} %fusion.127), channel_id=1, source_target_pairs={{0,14},{2,0},{4,2},{6,4},{8,6},{10,8},{12,10},{14,12},{1,15},{3,1}... | collective-permute-start | bytes 614408 | tf_op jit(solution)/shard_map/ppermute | solution.py:11
  145.4 16.1 %collective-permute-start.1 = (f32[400,256]{0,1:T(8,128)S(1)}, f32[400,256]{0,1:T(8,128)S(1)}, u32[]{:S(2)}, u32[]{:S(2)}) collective-permute-start(f32[400,256]{0,1:T(8,128)S(1)} %scatter_fusion.1), channel_id=1, source_target_pairs={{0,2},{2,4},{4,6},{6,8},{8,10},{10,12},{12,14},{14,0},{1,3},{3,5},... | collective-permute-start | bytes 1228808 | tf_op jit(solution)/shard_map/ppermute | solution.py:11
  146.9 14.6 %copy-start.103 = (s32[512,1]{0,1:T(1,128)S(1)}, s32[512,1]{0,1:T(1,128)}, u32[]{:S(2)}) copy-start(s32[512,1]{0,1:T(1,128)} %compare_select_fusion.18) | copy-start | bytes 6148
  166.2 19.4 %copy-start.7 = (f32[400,256]{0,1:T(8,128)S(1)}, f32[400,256]{0,1:T(8,128)}, u32[]{:S(2)}) copy-start(f32[400,256]{0,1:T(8,128)} %copy-done.6) | copy-start | bytes 1228804
  167.0 91.9 %all-reduce.12.cloned.1.call-start = ((), (), s32[]{:S(2)}) async-start(), calls=%async_computation.2 | async-start | bytes 1048576 | tf_op jit(solution)/shard_map/psum | solution.py:114
  187.8 9.6 %collective-permute-start.2 = (bf16[400,256]{0,1:T(8,128)(2,1)S(1)}, bf16[400,256]{0,1:T(8,128)(2,1)S(1)}, u32[]{:S(2)}, u32[]{:S(2)}) collective-permute-start(bf16[400,256]{0,1:T(8,128)(2,1)S(1)} %get-tuple-element.36), channel_id=1, source_target_pairs={{0,12},{2,14},{4,0},{6,2},{8,4},{10,6},{12,8},{14,10},{1,13},{3,15... | collective-permute-start | bytes 614408 | tf_op jit(solution)/shard_map/ppermute | solution.py:11
  219.5 15.9 %collective-permute-start.3 = (f32[400,256]{0,1:T(8,128)S(1)}, f32[400,256]{0,1:T(8,128)S(1)}, u32[]{:S(2)}, u32[]{:S(2)}) collective-permute-start(f32[400,256]{0,1:T(8,128)S(1)} %scatter_fusion.3), channel_id=1, source_target_pairs={{0,4},{2,6},{4,8},{6,10},{8,12},{10,14},{12,0},{14,2},{1,5},{3,7},... | collective-permute-start | bytes 1228808 | tf_op jit(solution)/shard_map/ppermute | solution.py:11
  221.7 13.8 %copy-start.102 = (s32[512,1]{0,1:T(1,128)S(1)}, s32[512,1]{0,1:T(1,128)}, u32[]{:S(2)}) copy-start(s32[512,1]{0,1:T(1,128)} %compare_select_fusion.15) | copy-start | bytes 6148
  239.9 20.1 %copy-start.88 = (f32[256]{0:T(256)S(1)}, f32[256]{0:T(256)}, u32[]{:S(2)}) copy-start(f32[256]{0:T(256)} %get-tuple-element.39) | copy-start | bytes 3076
  240.0 26.6 %copy-start.82 = (s32[1024]{0:T(1024)S(1)}, s32[1024]{0:T(1024)}, u32[]{:S(2)}) copy-start(s32[1024]{0:T(1024)} %pad_clamp_fusion.11) | copy-start | bytes 12292
  240.7 107.4 %all-reduce.14.cloned.1.call-start = ((), (), s32[]{:S(2)}) async-start(), calls=%async_computation.3 | async-start | bytes 1048576 | tf_op jit(solution)/shard_map/psum | solution.py:114
  247.2 25.2 %copy-start.9 = (f32[400,4,128]{2,0,1:T(8,128)}, f32[400,4,128]{2,0,1:T(8,128)S(1)}, u32[]{:S(2)}) copy-start(f32[400,4,128]{2,0,1:T(8,128)S(1)} %bitcast_bitcast_fusion.22) | copy-start | bytes 2457604
  262.5 11.4 %collective-permute-start.4 = (bf16[400,256]{0,1:T(8,128)(2,1)S(1)}, bf16[400,256]{0,1:T(8,128)(2,1)S(1)}, u32[]{:S(2)}, u32[]{:S(2)}) collective-permute-start(bf16[400,256]{0,1:T(8,128)(2,1)S(1)} %fusion.128), channel_id=1, source_target_pairs={{0,10},{2,12},{4,14},{6,0},{8,2},{10,4},{12,6},{14,8},{1,11},{3,13... | collective-permute-start | bytes 614408 | tf_op jit(solution)/shard_map/ppermute | solution.py:11
  296.9 26.9 %collective-permute-start.5 = (f32[400,256]{0,1:T(8,128)S(1)}, f32[400,256]{0,1:T(8,128)S(1)}, u32[]{:S(2)}, u32[]{:S(2)}) collective-permute-start(f32[400,256]{0,1:T(8,128)S(1)} %scatter_fusion.5), channel_id=1, source_target_pairs={{0,6},{2,8},{4,10},{6,12},{8,14},{10,0},{12,2},{14,4},{1,7},{3,9},... | collective-permute-start | bytes 1228808 | tf_op jit(solution)/shard_map/ppermute | solution.py:11
  300.5 23.4 %copy-start.101 = (s32[512,1]{0,1:T(1,128)S(1)}, s32[512,1]{0,1:T(1,128)}, u32[]{:S(2)}) copy-start(s32[512,1]{0,1:T(1,128)} %compare_select_fusion.12) | copy-start | bytes 6148
  328.5 20.8 %copy-start.79 = (f32[256]{0:T(256)S(1)}, f32[256]{0:T(256)}, u32[]{:S(2)}) copy-start(f32[256]{0:T(256)} %copy-done.78) | copy-start | bytes 3076
  328.5 20.8 %copy-start.89 = (f32[256]{0:T(256)S(1)}, f32[256]{0:T(256)}, u32[]{:S(2)}) copy-start(f32[256]{0:T(256)} %get-tuple-element.39) | copy-start | bytes 3076
  328.6 21.3 %copy-start.91 = (f32[256]{0:T(256)S(1)}, f32[256]{0:T(256)}, u32[]{:S(2)}) copy-start(f32[256]{0:T(256)} %copy-done.90) | copy-start | bytes 3076
  329.3 109.0 %all-reduce.16.cloned.1.call-start = ((), (), s32[]{:S(2)}) async-start(), calls=%async_computation.4 | async-start | bytes 1048576 | tf_op jit(solution)/shard_map/psum | solution.py:114
  331.9 23.0 %copy-start.81 = (s32[1024]{0:T(1024)S(1)}, s32[1024]{0:T(1024)}, u32[]{:S(2)}) copy-start(s32[1024]{0:T(1024)} %pad_clamp_fusion.7) | copy-start | bytes 12292
  336.3 24.3 %copy-start.8 = (f32[400,4,128]{2,0,1:T(8,128)}, f32[400,4,128]{2,0,1:T(8,128)S(1)}, u32[]{:S(2)}) copy-start(f32[400,4,128]{2,0,1:T(8,128)S(1)} %bitcast_bitcast_fusion.20) | copy-start | bytes 2457604
  352.3 15.1 %copy-start.83 = (s32[1024]{0:T(1024)S(1)}, s32[1024]{0:T(1024)}, u32[]{:S(2)}) copy-start(s32[1024]{0:T(1024)} %pad_clamp_fusion.5) | copy-start | bytes 12292
  352.3 15.1 %collective-permute-start.6 = (bf16[400,256]{0,1:T(8,128)(2,1)S(1)}, bf16[400,256]{0,1:T(8,128)(2,1)S(1)}, u32[]{:S(2)}, u32[]{:S(2)}) collective-permute-start(bf16[400,256]{0,1:T(8,128)(2,1)S(1)} %get-tuple-element.32), channel_id=1, source_target_pairs={{0,8},{2,10},{4,12},{6,14},{8,0},{10,2},{12,4},{14,6},{1,9},{3,11}... | collective-permute-start | bytes 614408 | tf_op jit(solution)/shard_map/ppermute | solution.py:11
  362.4 12.9 %copy-start.59 = (f32[4,128]{1,0:T(4,128)S(1)}, f32[4,128]{1,0:T(4,128)}, u32[]{:S(2)}) copy-start(f32[4,128]{1,0:T(4,128)} %get-tuple-element.143) | copy-start | bytes 6148
  362.4 12.9 %copy-start.140 = (f32[4,128]{1,0:T(4,128)S(1)}, f32[4,128]{1,0:T(4,128)}, u32[]{:S(2)}) copy-start(f32[4,128]{1,0:T(4,128)} %gather_fusion.29) | copy-start | bytes 6148
  389.2 25.5 %collective-permute-start.7 = (f32[400,256]{0,1:T(8,128)S(1)}, f32[400,256]{0,1:T(8,128)S(1)}, u32[]{:S(2)}, u32[]{:S(2)}) collective-permute-start(f32[400,256]{0,1:T(8,128)S(1)} %scatter_fusion.7), channel_id=1, source_target_pairs={{0,8},{2,10},{4,12},{6,14},{8,0},{10,2},{12,4},{14,6},{1,9},{3,11}... | collective-permute-start | bytes 1228808 | tf_op jit(solution)/shard_map/ppermute | solution.py:11
  390.8 24.0 %copy-start.100 = (s32[512,1]{0,1:T(1,128)S(1)}, s32[512,1]{0,1:T(1,128)}, u32[]{:S(2)}) copy-start(s32[512,1]{0,1:T(1,128)} %compare_select_fusion.9) | copy-start | bytes 6148
  420.1 107.3 %all-reduce.18.cloned.1.call-start = ((), (), s32[]{:S(2)}) async-start(), calls=%async_computation.5 | async-start | bytes 1048576 | tf_op jit(solution)/shard_map/psum | solution.py:114
  430.5 12.6 %copy-start.85 = (s32[1024]{0:T(1024)S(1)}, s32[1024]{0:T(1024)}, u32[]{:S(2)}) copy-start(s32[1024]{0:T(1024)} %pad_clamp_fusion.3) | copy-start | bytes 12292
  440.7 15.7 %collective-permute-start.8 = (bf16[400,256]{0,1:T(8,128)(2,1)S(1)}, bf16[400,256]{0,1:T(8,128)(2,1)S(1)}, u32[]{:S(2)}, u32[]{:S(2)}) collective-permute-start(bf16[400,256]{0,1:T(8,128)(2,1)S(1)} %fusion.129), channel_id=1, source_target_pairs={{0,6},{2,8},{4,10},{6,12},{8,14},{10,0},{12,2},{14,4},{1,7},{3,9},... | collective-permute-start | bytes 614408 | tf_op jit(solution)/shard_map/ppermute | solution.py:11
  445.2 15.1 %copy-start.114 = (s32[4]{0:T(128)S(1)}, s32[4]{0:T(128)}, u32[]{:S(2)}) copy-start(s32[4]{0:T(128)} %get-tuple-element.22) | copy-start | bytes 52
  475.3 13.9 %collective-permute-start.9 = (f32[400,256]{0,1:T(8,128)S(1)}, f32[400,256]{0,1:T(8,128)S(1)}, u32[]{:S(2)}, u32[]{:S(2)}) collective-permute-start(f32[400,256]{0,1:T(8,128)S(1)} %scatter_fusion.9), channel_id=1, source_target_pairs={{0,10},{2,12},{4,14},{6,0},{8,2},{10,4},{12,6},{14,8},{1,11},{3,13... | collective-permute-start | bytes 1228808 | tf_op jit(solution)/shard_map/ppermute | solution.py:11
  476.8 12.5 %copy-start.97 = (s32[512,1]{0,1:T(1,128)S(1)}, s32[512,1]{0,1:T(1,128)}, u32[]{:S(2)}) copy-start(s32[512,1]{0,1:T(1,128)} %compare_select_fusion.6) | copy-start | bytes 6148
  493.9 152.2 %all-reduce.20.cloned.1.call-start = ((), (), s32[]{:S(2)}) async-start(), calls=%async_computation.6 | async-start | bytes 8388608 | tf_op jit(solution)/shard_map/psum | solution.py:116
  527.3 121.5 %copy-start.134 = (f32[2048]{0:T(1024)S(1)}, f32[2048]{0:T(1024)}, u32[]{:S(2)}) copy-start(f32[2048]{0:T(1024)} %param.12) | copy-start | bytes 24580
  (102 other events, 501.1 us)
Sparse Core Ops, SparseCore 0:
  79.7 21.4 all-reduce.7
  167.1 16.0 all-reduce.9
  240.8 18.0 all-reduce.11
  329.4 18.6 all-reduce.13
  420.2 17.6 all-reduce.15
  494.0 25.8 all-reduce.17
  527.5 118.6 all-reduce.19
where the time goes:
time: 678 us; the launch traced here: 667 us
  other arithmetic  229 us (34%)
  waiting for transfers between devices  226 us (33%)
  local copies, waits for them, and re-layouts  149 us (22%)
  matrix products  22.9 us (3%)
  starting transfers between devices  22.4 us (3%)
  between operations  16.7 us (2%)
    psum x1, waiting for transfers between devices, on_device(): total_rel = lax.psum(rel_grad, ('dom', 'edge'))  115 us
    ppermute x10, waiting for transfers between devices, passed_along(): lax.ppermute(shard, axis, [(i, (i + by) % devices) for i in range(devices)])  78.6 us
    scatter-add x6, other arithmetic, block_terms(): rel_total.at[:, rel_idx.reshape(-1)].add(drelation.reshape(width, -1))  45.6 us
    psum x6, waiting for transfers between devices, on_device(): total = lax.psum(grad_src + returned, 'edge')  32.9 us
    unnamed x308, local copies, waits for them, and re-layouts  29.6 us
    scatter-add x6, other arithmetic, block_terms(): grad_dst.at[:, dst_idx[negative].reshape(-1)].add(dneg.reshape(width, -1))  27.5 us
    scatter-add x6, other arithmetic, block_terms(): grad_src = jnp.zeros((width, rows), jnp.float32).at[:, src_idx.reshape(-1...  27.2 us
    scatter-add x6, other arithmetic, block_terms(): grad_dst = jnp.zeros((width, rows), jnp.float32).at[:, dst_idx.reshape(-1...  26.3 us
  transfers between devices with their start and end apart: 17, of which 12 were waited for; matrix products, arithmetic and copies ran while one was open for 25% of the time, Pallas kernels for 0%

commit v1 on v0

v1 whole, which is shorter than its diff:
```python
import functools

import jax
import jax.numpy as jnp
from jax import lax
from jax.experimental import pallas as pl
from jax.experimental.pallas import tpu as pltpu
from jax.sharding import PartitionSpec as P

learn_rate = 0.1
BF = jnp.bfloat16
F32 = jnp.float32
VMEM_LIMIT = 40 * 1024 * 1024
NN = (((1,), (0,)), ((), ()))
NT = (((1,), (1,)), ((), ()))
TN = (((0,), (0,)), ((), ()))


def mm(a, b, dims=NN):
    return lax.dot_general(a, b, dims, preferred_element_type=F32)


def vmem():
    return pl.BlockSpec(memory_space=pltpu.VMEM)


def smem():
    return pl.BlockSpec(memory_space=pltpu.SMEM)


def cost(flops, size):
    return pl.CostEstimate(flops=flops, bytes_accessed=size, transcendentals=0)


def params():
    return pltpu.CompilerParams(vmem_limit_bytes=VMEM_LIMIT)


def shifted(x, by):
    n = lax.axis_size("dom")
    return lax.ppermute(x, "dom", [(i, (i + by) % n) for i in range(n)])


def across(x):
    return lax.ppermute(x, "edge", [(0, 1), (1, 0)])


def shifted_across(x, by):
    n = lax.axis_size("dom")
    pairs = [(2 * i + c, 2 * ((i + by) % n) + 1 - c) for i in range(n) for c in range(2)]
    return lax.ppermute(x, ("dom", "edge"), pairs)


def one_hot(rows_ref, t, count, base):
    blocks, width = rows_ref.shape[1:]
    at = lax.broadcasted_iota(jnp.int32, (count, width), 0)
    idx = rows_ref[t]
    return jnp.concatenate(
        [
            jnp.where(at == base(idx[b : b + 1, :]), 1.0, 0.0).astype(BF)
            for b in range(blocks)
        ],
        axis=1,
    )


def relvec_kernel(t, ids_ref, rel_ref, out_ref, acc):
    step = pl.program_id(0)
    tile = rel_ref.shape[1]
    hot = one_hot(ids_ref, t, tile, lambda i: i - step * tile)
    part = mm(rel_ref[...].astype(BF), hot)

    @pl.when(step == 0)
    def _():
        acc[...] = part

    @pl.when(step > 0)
    def _():
        acc[...] += part

    @pl.when(step == pl.num_programs(0) - 1)
    def _():
        out_ref[...] = acc[...].astype(BF)


def relvec(t, rel_ids, relations):
    width, rels = relations.shape
    slots = rel_ids.shape[1] * rel_ids.shape[2]
    tile = min(rels, 512)
    return pl.pallas_call(
        functools.partial(relvec_kernel, t),
        grid=(rels // tile,),
        in_specs=[
            pl.BlockSpec(rel_ids.shape, lambda i: (0, 0, 0)),
            pl.BlockSpec((width, tile), lambda i: (0, i)),
        ],
        out_specs=pl.BlockSpec((width, slots), lambda i: (0, 0)),
        out_shape=jax.ShapeDtypeStruct((width, slots), BF),
        scratch_shapes=[pltpu.VMEM((width, slots), F32)],
        compiler_params=params(),
        cost_estimate=cost(2 * width * rels * slots, 4 * width * rels),
        name="relvec",
    )(rel_ids, relations)


def relsum_kernel(t, first, ids_ref, drel_ref, *refs):
    step = pl.program_id(0)
    out_ref = refs[-1]
    tile = out_ref.shape[1]
    hot = one_hot(ids_ref, t, tile, lambda i: i - step * tile)
    part = mm(drel_ref[...], hot, NT)
    out_ref[...] = part if first else refs[0][...] + part


def relsum(t, rel_ids, drel, acc, rels):
    width, slots = drel.shape
    tile = min(rels, 512)
    wide = pl.BlockSpec((width, tile), lambda i: (0, i))
    ins = [rel_ids, drel] + ([] if acc is None else [acc])
    return pl.pallas_call(
        functools.partial(relsum_kernel, t, acc is None),
        grid=(rels // tile,),
        in_specs=[
            pl.BlockSpec(rel_ids.shape, lambda i: (0, 0, 0)),
            pl.BlockSpec((width, slots), lambda i: (0, 0)),
        ]
        + ([] if acc is None else [wide]),
        out_specs=wide,
        out_shape=jax.ShapeDtypeStruct((width, rels), F32),
        input_output_aliases={} if acc is None else {2: 0},
        compiler_params=params(),
        cost_estimate=cost(2 * width * rels * slots, 8 * width * rels),
        name="relsum",
    )(*ins)


def edge_kernel(t, me_ref, src_ref, dst_ref, cnt_ref, neg_ref, rel_ref, *refs):
    first = t == 0
    blocks, width = src_ref.shape[1:]
    if first:
        (ent_ref, g_mine, g_other, drel_ref, o_scr, d_scr) = refs
        half = ent_ref.shape[1] // 2
    else:
        (own0, own1, far0, far1, gs_mine, gs_other, gd_mine, gd_other, drel_ref, o_scr, d_scr) = refs
        half = own0.shape[1]
    rows = 2 * half
    edge = me_ref[1]
    dim = o_scr.shape[0]
    hd = dim // 2

    if first:
        table = jnp.concatenate(
            [
                ent_ref[:, pl.ds(pl.multiple_of(h * half, half), half)].astype(BF)
                for h in (edge, 1 - edge)
            ],
            axis=1,
        )
        far = table
    else:
        table = jnp.concatenate([own0[...], own1[...]], axis=1)
        far = jnp.concatenate([far0[...], far1[...]], axis=1)

    def local(idx):
        moved = idx + edge * half
        return jnp.where(moved >= rows, moved - rows, moved)

    s_hot = one_hot(src_ref, t, rows, local)
    d_hot = one_hot(dst_ref, t, rows, local)
    source = mm(table, s_hot)
    target = mm(far, d_hot)
    o_scr[...] = target.astype(BF)
    rel = rel_ref[...].astype(F32)
    s_re, s_im, w_re, w_im = source[:hd], source[hd:], rel[:hd], rel[hd:]
    query = jnp.concatenate([s_re * w_re - s_im * w_im, s_re * w_im + s_im * w_re], axis=0).astype(BF)
    query_f = query.astype(F32)
    pos = jnp.sum(query_f * target, axis=0, keepdims=True)
    lane = lax.broadcasted_iota(jnp.int32, (1, width), 1)
    valid = jnp.concatenate(
        [jnp.where(lane < cnt_ref[t, b], 1.0, 0.0) for b in range(blocks)], axis=1
    )
    gpos = -jax.nn.sigmoid(-pos) * valid
    d_scr[...] = gpos * query_f
    row_j = lax.broadcasted_iota(jnp.int32, (width, width), 0)
    col_i = lax.broadcasted_iota(jnp.int32, (width, width), 1)
    dq = []
    for b in range(blocks):
        lo = b * width
        nb = neg_ref[t, b]
        at = pl.ds(pl.multiple_of(nb * width, width), width)
        neg = o_scr[:, at]
        qb = query[:, lo : lo + width]
        scores = mm(neg, qb, TN)
        keep = jnp.logical_and(row_j < cnt_ref[t, nb], col_i < cnt_ref[t, b])
        weight = jnp.where(keep, jax.nn.sigmoid(scores) / width, 0.0).astype(BF)
        dq.append(gpos[:, lo : lo + width] * target[:, lo : lo + width] + mm(neg, weight))
        d_scr[:, at] += mm(qb, weight, NT)
    dq = jnp.concatenate(dq, axis=1)
    dq_re, dq_im = dq[:hd], dq[hd:]
    drel_ref[...] = jnp.concatenate(
        [dq_re * s_re + dq_im * s_im, dq_im * s_re - dq_re * s_im], axis=0
    ).astype(BF)
    dsource = jnp.concatenate(
        [dq_re * w_re + dq_im * w_im, dq_im * w_re - dq_re * w_im], axis=0
    ).astype(BF)
    gs = mm(dsource, s_hot, NT)
    gd = mm(d_scr[...].astype(BF), d_hot, NT)
    if first:
        total = gs + gd
        g_mine[...] = total[:, :half]
        g_other[...] = total[:, half:].astype(BF)
    else:
        gs_mine[...] = gs[:, :half]
        gs_other[...] = gs[:, half:].astype(BF)
        gd_mine[...] = gd[:, :half].astype(BF)
        gd_other[...] = gd[:, half:].astype(BF)


def edge_round(t, me, src, dst, cnt, neg, rel, tables):
    dim, slots = rel.shape
    rows = sum(x.shape[1] for x in tables[:2])
    half = rows // 2
    lo = jax.ShapeDtypeStruct((dim, half), BF)
    hi = jax.ShapeDtypeStruct((dim, half), F32)
    outs = ([hi, lo] if t == 0 else [hi, lo, lo, lo]) + [jax.ShapeDtypeStruct((dim, slots), BF)]
    return pl.pallas_call(
        functools.partial(edge_kernel, t),
        in_specs=[smem(), vmem(), vmem(), smem(), smem(), vmem()] + [vmem()] * len(tables),
        out_specs=[vmem()] * len(outs),
        out_shape=outs,
        scratch_shapes=[pltpu.VMEM((dim, slots), BF), pltpu.VMEM((dim, slots), F32)],
        compiler_params=params(),
        cost_estimate=cost(8 * dim * rows * slots, 12 * dim * slots),
        name="edges",
    )(me, src, dst, cnt, neg, rel, *tables)


def update_kernel(t, me_ref, ent_ref, state_ref, *refs):
    grads, (ent_out, state_out, low_out) = refs[:-3], refs[-3:]
    half = ent_out.shape[1]
    if t == 0:
        at = pl.ds(pl.multiple_of(me_ref[1] * half, half), half)
        ent, state = ent_ref[:, at], state_ref[:, at]
    else:
        ent, state = ent_ref[...], state_ref[...]
    grad = grads[0][...].astype(F32)
    for g in grads[1:]:
        grad = grad + g[...].astype(F32)
    state = state + jnp.sum(grad * grad, axis=0, keepdims=True) / grad.shape[0]
    new = ent - learn_rate * grad / jnp.sqrt(state)
    ent_out[...] = new
    state_out[...] = state
    low_out[...] = new.astype(BF)


def update(t, me, ent, state, grads):
    dim, half = grads[0].shape
    return pl.pallas_call(
        functools.partial(update_kernel, t),
        in_specs=[smem()] + [vmem()] * (2 + len(grads)),
        out_specs=[vmem()] * 3,
        out_shape=[
            jax.ShapeDtypeStruct((dim, half), F32),
            jax.ShapeDtypeStruct((1, half), F32),
            jax.ShapeDtypeStruct((dim, half), BF),
        ],
        compiler_params=params(),
        cost_estimate=cost(10 * dim * half, 16 * dim * half),
        name="update",
    )(me, ent, state, *grads)


def pieces_kernel(t, n, me_ref, ids_ref, drel_ref, acc_ref, *refs):
    outs, total = refs[:-1], refs[-1]
    slots = drel_ref.shape[1]
    rels = total.shape[1]
    tile = min(rels, 512)
    drel = drel_ref[...]
    for lo in range(0, rels, tile):
        hot = one_hot(ids_ref, t, tile, lambda i, lo=lo: i - lo)
        total[:, lo : lo + tile] = acc_ref[:, lo : lo + tile] + mm(drel, hot, NT)
    w = outs[0].shape[1]
    for k in range(n):
        owner = lax.rem(me_ref[0] + k, n)
        for c in range(2):
            core = me_ref[1] if c == 0 else 1 - me_ref[1]
            at = pl.ds(pl.multiple_of((2 * owner + core) * w, w), w)
            outs[c * n + k][...] = total[:, at].astype(BF)


def pieces(t, n, me, rel_ids, drel, acc):
    dim, rels = acc.shape
    w = rels // (2 * n)
    return pl.pallas_call(
        functools.partial(pieces_kernel, t, n),
        in_specs=[smem()] + [vmem()] * 3,
        out_specs=[vmem()] * (2 * n),
        out_shape=[jax.ShapeDtypeStruct((dim, w), BF)] * (2 * n),
        scratch_shapes=[pltpu.VMEM((dim, rels), F32)],
        compiler_params=params(),
        cost_estimate=cost(2 * dim * rels * drel.shape[1], 8 * dim * rels),
        name="pieces",
    )(me, rel_ids, drel, acc)


def add_kernel(n, *refs):
    for k in range(n):
        refs[2 * n + k][...] = (refs[k][...].astype(F32) + refs[n + k][...].astype(F32)).astype(BF)


def add_pairs(mine, theirs):
    n = len(mine)
    return pl.pallas_call(
        functools.partial(add_kernel, n),
        in_specs=[vmem()] * (2 * n),
        out_specs=[vmem()] * n,
        out_shape=[jax.ShapeDtypeStruct(x.shape, BF) for x in mine],
        compiler_params=params(),
        name="add_pairs",
    )(*mine, *theirs)


def sum_kernel(*refs):
    total = refs[0][...].astype(F32)
    for r in refs[1:-1]:
        total = total + r[...].astype(F32)
    refs[-1][...] = total.astype(BF)


def sum_all(parts):
    return pl.pallas_call(
        sum_kernel,
        in_specs=[vmem()] * len(parts),
        out_specs=vmem(),
        out_shape=jax.ShapeDtypeStruct(parts[0].shape, BF),
        compiler_params=params(),
        name="sum_all",
    )(*parts)


def relnew_kernel(n, me_ref, rel_ref, state_ref, *refs):
    got, (rel_out, state_out) = refs[:-2], refs[-2:]
    w = got[0].shape[1]
    for k in range(n):
        owner = lax.rem(me_ref[0] + n - k, n)
        for c in range(2):
            core = me_ref[1] if c == 0 else 1 - me_ref[1]
            at = pl.ds(pl.multiple_of((2 * owner + core) * w, w), w)
            grad = got[c * n + k][...].astype(F32)
            state = state_ref[:, at] + jnp.sum(grad * grad, axis=0, keepdims=True) / grad.shape[0]
            state_out[:, at] = state
            rel_out[:, at] = rel_ref[:, at] - learn_rate * grad / jnp.sqrt(state)


def relnew(n, me, relations, state, got):
    dim, rels = relations.shape
    return pl.pallas_call(
        functools.partial(relnew_kernel, n),
        in_specs=[smem()] + [vmem()] * (2 + len(got)),
        out_specs=[vmem()] * 2,
        out_shape=[jax.ShapeDtypeStruct((dim, rels), F32), jax.ShapeDtypeStruct((1, rels), F32)],
        compiler_params=params(),
        name="relnew",
    )(me, relations, state, *got)


def relation_update(t, me, rel_ids, drel, acc, relations, state):
    n = lax.axis_size("dom")
    dim, rels = relations.shape
    if rels % (256 * n):
        total = relsum(t, rel_ids, drel, acc, rels)
        total = lax.psum(total, ("dom", "edge"))
        state = state + jnp.mean(total * total, axis=0)
        return relations - learn_rate * total / jnp.sqrt(state)[None, :], state
    parts = pieces(t, n, me, rel_ids, drel, acc)
    mine, other = parts[:n], parts[n:]
    theirs = [across(x) for x in other]
    mine = add_pairs(mine, theirs)
    summed = sum_all([mine[0]] + [shifted(mine[k], k) for k in range(1, n)])
    got = [summed] + [shifted(summed, k) for k in range(1, n)]
    got = got + [across(x) for x in got]
    rel_new, state_new = relnew(n, me, relations, state.reshape(1, rels), got)
    return rel_new, state_new.reshape(rels)


def on_device(
    entities,
    entity_state,
    relations,
    relation_state,
    src_rows,
    rel_ids,
    dst_rows,
    counts,
    neg_blocks,
):
    rounds = src_rows.shape[0]
    rels = relations.shape[1]
    me = jnp.stack([lax.axis_index("dom"), lax.axis_index("edge")]).astype(jnp.int32)
    ent, state = entities, entity_state.reshape(1, -1)
    tables = (entities,) * 1
    acc = None
    for t in range(rounds):
        rel = relvec(t, rel_ids, relations)
        if t == 0:
            g_mine, g_other, drel = edge_round(t, me, src_rows, dst_rows, counts, neg_blocks, rel, tables)
            grads = [g_mine, across(g_other)]
        else:
            gs_mine, gs_other, gd_mine, gd_other, drel = edge_round(
                t, me, src_rows, dst_rows, counts, neg_blocks, rel, tables
            )
            grads = [gs_mine, across(gs_other), shifted(gd_mine, t), shifted_across(gd_other, t)]
        if t < rounds - 1:
            acc = relsum(t, rel_ids, drel, acc, rels)
        ent, state, low = update(t, me, ent, state, grads)
        if t < rounds - 1:
            tables = (low, across(low), shifted(low, -t - 1), shifted_across(low, -t - 1))
    rel_new, rel_state = relation_update(
        rounds - 1, me, rel_ids, drel, acc, relations, relation_state
    )
    first = lax.axis_index("edge") == 0
    ent_there, state_there = across(ent), across(state)
    ent = jnp.where(
        first,
        jnp.concatenate([ent, ent_there], axis=1),
        jnp.concatenate([ent_there, ent], axis=1),
    )
    state = jnp.where(
        first,
        jnp.concatenate([state, state_there], axis=1),
        jnp.concatenate([state_there, state], axis=1),
    )
    return (ent, state.reshape(-1), rel_new, rel_state)


def solution(mesh):
    return jax.shard_map(
        on_device,
        mesh=mesh,
        in_specs=(
            P(None, ("groups", "dom")),
            P(("groups", "dom")),
            P(None, "groups"),
            P("groups"),
            P(None, ("groups", "dom", "edge"), None),
            P(None, ("groups", "dom", "edge"), None),
            P(None, ("groups", "dom", "edge"), None),
            P(None, ("groups", "dom", "edge")),
            P(None, ("groups", "dom", "edge")),
        ),
        out_specs=(
            P(None, ("groups", "dom")),
            P(("groups", "dom")),
            P(None, "groups"),
            P("groups"),
        ),
        check_vma=False,
    )
```

time: 678 us -> 191 us (0.28)
  the two profiles are of different devices: /device:TPU:0 before, /device:TPU:15 now
where the time goes in v1:
time: 191 us; the launch traced here: 190 us
  starting transfers between devices  83.4 us (44%)
  Pallas kernels  52.7 us (28%)
  waiting for transfers between devices  44.8 us (23%)
  local copies, waits for them, and re-layouts  5.76 us (3%)
  other arithmetic  2.67 us (1%)
    ppermute x24, starting transfers between devices, shifted(): return lax.ppermute(x, 'dom', [(i, (i + by) % n) for i in range(n)])  41.5 us
    ppermute x10, starting transfers between devices, shifted_across(): return lax.ppermute(x, ('dom', 'edge'), pairs)  27 us
    ppermute x10, waiting for transfers between devices, shifted_across(): return lax.ppermute(x, ('dom', 'edge'), pairs)  23.1 us
    ppermute x24, waiting for transfers between devices, shifted(): return lax.ppermute(x, 'dom', [(i, (i + by) % n) for i in range(n)])  19.6 us
    pallas_call x6, Pallas kernels, edge_round(): pl.pallas_call(functools.partial(edge_kernel, t), in_specs=[smem(), vmem(...  18.3 us
    ppermute x29, starting transfers between devices, across(): return lax.ppermute(x, 'edge', [(0, 1), (1, 0)])  14.9 us
    pallas_call x6, Pallas kernels, relvec(): pl.pallas_call(functools.partial(relvec_kernel, t), grid=(rels // tile,),...  12.7 us
    pallas_call x5, Pallas kernels, relsum(): pl.pallas_call(functools.partial(relsum_kernel, t, acc is None), grid=(re...  10.7 us
  transfers between devices with their start and end apart: 63, of which 24 were waited for; matrix products, arithmetic and copies ran while one was open for 1% of the time, Pallas kernels for 12%

profile of v1, /device:TPU:15, one launch (start us, length us, event | category | flops | bytes accessed | tf_op | source)
XLA Modules:
  0.0 190.3 jit_solution(8244241634365225585)
XLA Ops:
  2.3 1.9 %copy-done = f32[400,2048]{1,0:T(8,128)S(1)} copy-done((f32[400,2048]{1,0:T(8,128)S(1)}, f32[400,2048]{1,0:T(8,128)}, u32[]{:S(2)}) %copy-start) | copy-done | bytes 3276824
  4.9 2.1 %relvec.6.rel_ref = bf16[400,512]{1,0:T(8,128)(2,1)S(1)} custom-call(s32[6,4,128]{2,1,0:T(4,128)S(1)} %copy-done.2, f32[400,2048]{1,0:T(8,128)S(1)} %copy-done), custom_call_target="tpu_custom_call" | custom-call | flops 838860800 | bytes 3276800 | tf_op jit(solution)/shard_map/relvec/pallas_call | solution.py:90
  7.1 3.2 %edges.6 = (f32[400,128]{1,0:T(8,128)S(1)}, bf16[400,128]{1,0:T(8,128)(2,1)S(1)}, bf16[400,512]{1,0:T(8,128)(2,1)S(1)}) custom-call(s32[2]{0:T(128)S(1)} %pad_add_fusion.me_ref, s32[6,4,128]{2,1,0:T(4,128)S(1)} %copy-done.9, s32[6,4,128]{2,1,0:T(4,128)S(1)} %copy-done.10, s32[6,4]{1,0:T(8,128)S(1)} %copy.17.cnt_ref, s32[6,4]{1,0:T(8,128)S(1)} %copy.18.neg_ref, ...), custom_call_target="tpu_custom_call" | custom-call | flops 419430400 | bytes 2457600 | tf_op jit(solution)/shard_map/edges/pallas_call | solution.py:226
  11.1 0.9 collective-permute-done.refs_1_
  13.3 1.4 collective-permute-start.3
  14.8 2.1 %relvec.7.rel_ref = bf16[400,512]{1,0:T(8,128)(2,1)S(1)} custom-call(s32[6,4,128]{2,1,0:T(4,128)S(1)} %copy-done.3, f32[400,2048]{1,0:T(8,128)S(1)} %copy-done.1), custom_call_target="tpu_custom_call" | custom-call | flops 838860800 | bytes 3276800 | tf_op jit(solution)/shard_map/relvec/pallas_call | solution.py:90
  16.9 1.4 collective-permute-done.2.refs_2_
  18.3 2.5 %collective-permute-done.3.refs_3_ = bf16[400,128]{1,0:T(8,128)(2,1)S(1)} collective-permute-done((bf16[400,128]{1,0:T(8,128)(2,1)S(1)}, bf16[400,128]{1,0:T(8,128)(2,1)S(1)}, u32[]{:S(2)}, u32[]{:S(2)}) %collective-permute-start.3) | collective-permute-done | bytes 102432 | tf_op jit(solution)/shard_map/ppermute | solution.py:51
  20.8 3.0 %edges.7 = (f32[400,128]{1,0:T(8,128)S(1)}, bf16[400,128]{1,0:T(8,128)(2,1)S(1)}, bf16[400,128]{1,0:T(8,128)(2,1)S(1)}, bf16[400,128]{1,0:T(8,128)(2,1)S(1)}, bf16[400,512]{1,0:T(8,128)(2,1)S(1)}) custom-call(s32[2]{0:T(128)S(1)} %pad_add_fusion.me_ref, s32[6,4,128]{2,1,0:T(4,128)S(1)} %copy-done.9, s32[6,4,128]{2,1,0:T(4,128)S(1)} %copy-done.10, ...), custom_call_target="tpu_custom_call" | custom-call | flops 419430400 | bytes 2457600 | tf_op jit(solution)/shard_map/edges/pallas_call | solution.py:226
  24.4 2.7 %collective-permute-start.6 = (bf16[400,128]{1,0:T(8,128)(2,1)S(1)}, bf16[400,128]{1,0:T(8,128)(2,1)S(1)}, u32[]{:S(2)}, u32[]{:S(2)}) collective-permute-start(bf16[400,128]{1,0:T(8,128)(2,1)S(1)} %get-tuple-element.83), channel_id=1, source_target_pairs={{0,3},{1,2},{2,5},{3,4},{4,7},{5,6},{6,9},{7,8},{8,11},{9,10},{10,... | collective-permute-start | bytes 307208 | tf_op jit(solution)/shard_map/ppermute | solution.py:51
  27.0 1.0 collective-permute-done.5.refs_2_
  28.1 2.7 %collective-permute-done.6.refs_3_ = bf16[400,128]{1,0:T(8,128)(2,1)S(1)} collective-permute-done((bf16[400,128]{1,0:T(8,128)(2,1)S(1)}, bf16[400,128]{1,0:T(8,128)(2,1)S(1)}, u32[]{:S(2)}, u32[]{:S(2)}) %collective-permute-start.6) | collective-permute-done | bytes 102432 | tf_op jit(solution)/shard_map/ppermute | solution.py:51
  31.5 1.2 collective-permute-start.8
  32.7 4.8 %collective-permute-start.9 = (bf16[400,128]{1,0:T(8,128)(2,1)S(1)}, bf16[400,128]{1,0:T(8,128)(2,1)S(1)}, u32[]{:S(2)}, u32[]{:S(2)}) collective-permute-start(bf16[400,128]{1,0:T(8,128)(2,1)S(1)} %get-tuple-element.86.refs_0_), channel_id=1, source_target_pairs={{0,13},{1,12},{2,15},{3,14},{4,1},{5,0},{6,3},{7,2},{8,5},{9,4},{1... | collective-permute-start | bytes 307208 | tf_op jit(solution)/shard_map/ppermute | solution.py:51
  37.5 2.1 %relvec.8.rel_ref = bf16[400,512]{1,0:T(8,128)(2,1)S(1)} custom-call(s32[6,4,128]{2,1,0:T(4,128)S(1)} %copy-done.3, f32[400,2048]{1,0:T(8,128)S(1)} %copy-done.1), custom_call_target="tpu_custom_call" | custom-call | flops 838860800 | bytes 3276800 | tf_op jit(solution)/shard_map/relvec/pallas_call | solution.py:90
  40.2 3.0 %edges.8 = (f32[400,128]{1,0:T(8,128)S(1)}, bf16[400,128]{1,0:T(8,128)(2,1)S(1)}, bf16[400,128]{1,0:T(8,128)(2,1)S(1)}, bf16[400,128]{1,0:T(8,128)(2,1)S(1)}, bf16[400,512]{1,0:T(8,128)(2,1)S(1)}) custom-call(s32[2]{0:T(128)S(1)} %pad_add_fusion.me_ref, s32[6,4,128]{2,1,0:T(4,128)S(1)} %copy-done.9, s32[6,4,128]{2,1,0:T(4,128)S(1)} %copy-done.10, ...), custom_call_target="tpu_custom_call" | custom-call | flops 419430400 | bytes 2457600 | tf_op jit(solution)/shard_map/edges/pallas_call | solution.py:226
  43.6 0.9 collective-permute-start.11
  44.5 3.8 %collective-permute-start.12 = (bf16[400,128]{1,0:T(8,128)(2,1)S(1)}, bf16[400,128]{1,0:T(8,128)(2,1)S(1)}, u32[]{:S(2)}, u32[]{:S(2)}) collective-permute-start(bf16[400,128]{1,0:T(8,128)(2,1)S(1)} %get-tuple-element.90), channel_id=1, source_target_pairs={{0,5},{1,4},{2,7},{3,6},{4,9},{5,8},{6,11},{7,10},{8,13},{9,12},{1... | collective-permute-start | bytes 307208 | tf_op jit(solution)/shard_map/ppermute | solution.py:51
  49.0 2.2 %collective-permute-done.12.refs_3_ = bf16[400,128]{1,0:T(8,128)(2,1)S(1)} collective-permute-done((bf16[400,128]{1,0:T(8,128)(2,1)S(1)}, bf16[400,128]{1,0:T(8,128)(2,1)S(1)}, u32[]{:S(2)}, u32[]{:S(2)}) %collective-permute-start.12) | collective-permute-done | bytes 102432 | tf_op jit(solution)/shard_map/ppermute | solution.py:51
  52.3 3.7 %collective-permute-start.14 = (bf16[400,128]{1,0:T(8,128)(2,1)S(1)}, bf16[400,128]{1,0:T(8,128)(2,1)S(1)}, u32[]{:S(2)}, u32[]{:S(2)}) collective-permute-start(bf16[400,128]{1,0:T(8,128)(2,1)S(1)} %get-tuple-element.93.refs_0_), channel_id=1, source_target_pairs={{0,10},{2,12},{4,14},{6,0},{8,2},{10,4},{12,6},{14,8},{1,11},{3,13... | collective-permute-start | bytes 307208 | tf_op jit(solution)/shard_map/ppermute | solution.py:41
  56.7 2.1 %relvec.9.rel_ref = bf16[400,512]{1,0:T(8,128)(2,1)S(1)} custom-call(s32[6,4,128]{2,1,0:T(4,128)S(1)} %copy-done.3, f32[400,2048]{1,0:T(8,128)S(1)} %copy-done.1), custom_call_target="tpu_custom_call" | custom-call | flops 838860800 | bytes 3276800 | tf_op jit(solution)/shard_map/relvec/pallas_call | solution.py:90
  59.0 4.3 %collective-permute-done.15.refs_3_ = bf16[400,128]{1,0:T(8,128)(2,1)S(1)} collective-permute-done((bf16[400,128]{1,0:T(8,128)(2,1)S(1)}, bf16[400,128]{1,0:T(8,128)(2,1)S(1)}, u32[]{:S(2)}, u32[]{:S(2)}) %collective-permute-start.15) | collective-permute-done | bytes 102432 | tf_op jit(solution)/shard_map/ppermute | solution.py:51
  63.3 3.0 %edges.9 = (f32[400,128]{1,0:T(8,128)S(1)}, bf16[400,128]{1,0:T(8,128)(2,1)S(1)}, bf16[400,128]{1,0:T(8,128)(2,1)S(1)}, bf16[400,128]{1,0:T(8,128)(2,1)S(1)}, bf16[400,512]{1,0:T(8,128)(2,1)S(1)}) custom-call(s32[2]{0:T(128)S(1)} %pad_add_fusion.me_ref, s32[6,4,128]{2,1,0:T(4,128)S(1)} %copy-done.9, s32[6,4,128]{2,1,0:T(4,128)S(1)} %copy-done.10, ...), custom_call_target="tpu_custom_call" | custom-call | flops 419430400 | bytes 2457600 | tf_op jit(solution)/shard_map/edges/pallas_call | solution.py:226
  66.9 1.9 %collective-permute-start.17 = (bf16[400,128]{1,0:T(8,128)(2,1)S(1)}, bf16[400,128]{1,0:T(8,128)(2,1)S(1)}, u32[]{:S(2)}, u32[]{:S(2)}) collective-permute-start(bf16[400,128]{1,0:T(8,128)(2,1)S(1)} %get-tuple-element.96), channel_id=1, source_target_pairs={{0,6},{2,8},{4,10},{6,12},{8,14},{10,0},{12,2},{14,4},{1,7},{3,9},... | collective-permute-start | bytes 307208 | tf_op jit(solution)/shard_map/ppermute | solution.py:41
  68.8 5.3 %collective-permute-start.18 = (bf16[400,128]{1,0:T(8,128)(2,1)S(1)}, bf16[400,128]{1,0:T(8,128)(2,1)S(1)}, u32[]{:S(2)}, u32[]{:S(2)}) collective-permute-start(bf16[400,128]{1,0:T(8,128)(2,1)S(1)} %get-tuple-element.97), channel_id=1, source_target_pairs={{0,7},{1,6},{2,9},{3,8},{4,11},{5,10},{6,13},{7,12},{8,15},{9,14},... | collective-permute-start | bytes 307208 | tf_op jit(solution)/shard_map/ppermute | solution.py:51
  74.1 2.1 %relvec.10.rel_ref = bf16[400,512]{1,0:T(8,128)(2,1)S(1)} custom-call(s32[6,4,128]{2,1,0:T(4,128)S(1)} %copy-done.3, f32[400,2048]{1,0:T(8,128)S(1)} %copy-done.1), custom_call_target="tpu_custom_call" | custom-call | flops 838860800 | bytes 3276800 | tf_op jit(solution)/shard_map/relvec/pallas_call | solution.py:90
  76.2 2.6 %collective-permute-done.18.refs_3_ = bf16[400,128]{1,0:T(8,128)(2,1)S(1)} collective-permute-done((bf16[400,128]{1,0:T(8,128)(2,1)S(1)}, bf16[400,128]{1,0:T(8,128)(2,1)S(1)}, u32[]{:S(2)}, u32[]{:S(2)}) %collective-permute-start.18) | collective-permute-done | bytes 102432 | tf_op jit(solution)/shard_map/ppermute | solution.py:51
  80.1 2.5 %collective-permute-start.21 = (bf16[400,128]{1,0:T(8,128)(2,1)S(1)}, bf16[400,128]{1,0:T(8,128)(2,1)S(1)}, u32[]{:S(2)}, u32[]{:S(2)}) collective-permute-start(bf16[400,128]{1,0:T(8,128)(2,1)S(1)} %get-tuple-element.100.refs_0_), channel_id=1, source_target_pairs={{0,9},{1,8},{2,11},{3,10},{4,13},{5,12},{6,15},{7,14},{8,1},{9,0},... | collective-permute-start | bytes 307208 | tf_op jit(solution)/shard_map/ppermute | solution.py:51
  82.6 2.1 %relvec.11.rel_ref = bf16[400,512]{1,0:T(8,128)(2,1)S(1)} custom-call(s32[6,4,128]{2,1,0:T(4,128)S(1)} %copy-done.3, f32[400,2048]{1,0:T(8,128)S(1)} %copy-done.1), custom_call_target="tpu_custom_call" | custom-call | flops 838860800 | bytes 3276800 | tf_op jit(solution)/shard_map/relvec/pallas_call | solution.py:90
  84.7 1.9 %relsum.5.refs_0_ = f32[400,2048]{1,0:T(8,128)S(1)} custom-call(s32[6,4,128]{2,1,0:T(4,128)S(1)} %copy-done.3, bf16[400,512]{1,0:T(8,128)(2,1)S(1)} %get-tuple-element.119.drel_ref), custom_call_target="tpu_custom_call" | custom-call | flops 838860800 | bytes 6553600 | tf_op jit(solution)/shard_map/relsum/pallas_call | solution.py:120
  86.7 1.9 collective-permute-done.21.refs_3_
  88.6 3.0 %edges.10 = (f32[400,128]{1,0:T(8,128)S(1)}, bf16[400,128]{1,0:T(8,128)(2,1)S(1)}, bf16[400,128]{1,0:T(8,128)(2,1)S(1)}, bf16[400,128]{1,0:T(8,128)(2,1)S(1)}, bf16[400,512]{1,0:T(8,128)(2,1)S(1)}) custom-call(s32[2]{0:T(128)S(1)} %pad_add_fusion.me_ref, s32[6,4,128]{2,1,0:T(4,128)S(1)} %copy-done.9, s32[6,4,128]{2,1,0:T(4,128)S(1)} %copy-done.10, ...), custom_call_target="tpu_custom_call" | custom-call | flops 419430400 | bytes 2457600 | tf_op jit(solution)/shard_map/edges/pallas_call | solution.py:226
  91.6 1.3 collective-permute-start.22
  92.9 2.5 %collective-permute-start.23 = (bf16[400,128]{1,0:T(8,128)(2,1)S(1)}, bf16[400,128]{1,0:T(8,128)(2,1)S(1)}, u32[]{:S(2)}, u32[]{:S(2)}) collective-permute-start(bf16[400,128]{1,0:T(8,128)(2,1)S(1)} %get-tuple-element.103), channel_id=1, source_target_pairs={{0,8},{2,10},{4,12},{6,14},{8,0},{10,2},{12,4},{14,6},{1,9},{3,11}... | collective-permute-start | bytes 307208 | tf_op jit(solution)/shard_map/ppermute | solution.py:41
  95.7 2.2 %relsum.6.refs_0_ = f32[400,2048]{1,0:T(8,128)S(1)} custom-call(s32[6,4,128]{2,1,0:T(4,128)S(1)} %copy-done.3, bf16[400,512]{1,0:T(8,128)(2,1)S(1)} %get-tuple-element.118.drel_ref, f32[400,2048]{1,0:T(8,128)S(1)} %relsum.5.refs_0_), custom_call_target="tpu_custom_call", output_to_operand_aliasing={{}: (2, {})} | custom-call | flops 838860800 | bytes 6553600 | tf_op jit(solution)/shard_map/relsum/pallas_call | solution.py:120
  97.9 2.2 %relsum.7.refs_0_ = f32[400,2048]{1,0:T(8,128)S(1)} custom-call(s32[6,4,128]{2,1,0:T(4,128)S(1)} %copy-done.3, bf16[400,512]{1,0:T(8,128)(2,1)S(1)} %get-tuple-element.117.drel_ref, f32[400,2048]{1,0:T(8,128)S(1)} %relsum.6.refs_0_), custom_call_target="tpu_custom_call", output_to_operand_aliasing={{}: (2, {})} | custom-call | flops 838860800 | bytes 6553600 | tf_op jit(solution)/shard_map/relsum/pallas_call | solution.py:120
  100.1 3.6 %collective-permute-done.24.refs_3_ = bf16[400,128]{1,0:T(8,128)(2,1)S(1)} collective-permute-done((bf16[400,128]{1,0:T(8,128)(2,1)S(1)}, bf16[400,128]{1,0:T(8,128)(2,1)S(1)}, u32[]{:S(2)}, u32[]{:S(2)}) %collective-permute-start.24) | collective-permute-done | bytes 102432 | tf_op jit(solution)/shard_map/ppermute | solution.py:51
  104.4 1.3 collective-permute-start.25
  105.7 4.1 %collective-permute-start.26 = (bf16[400,128]{1,0:T(8,128)(2,1)S(1)}, bf16[400,128]{1,0:T(8,128)(2,1)S(1)}, u32[]{:S(2)}, u32[]{:S(2)}) collective-permute-start(bf16[400,128]{1,0:T(8,128)(2,1)S(1)} %get-tuple-element.107.refs_0_), channel_id=1, source_target_pairs={{0,6},{2,8},{4,10},{6,12},{8,14},{10,0},{12,2},{14,4},{1,7},{3,9},... | collective-permute-start | bytes 307208 | tf_op jit(solution)/shard_map/ppermute | solution.py:41
  109.8 1.3 collective-permute-start.27
  111.1 2.2 %relsum.8.refs_0_ = f32[400,2048]{1,0:T(8,128)S(1)} custom-call(s32[6,4,128]{2,1,0:T(4,128)S(1)} %copy-done.3, bf16[400,512]{1,0:T(8,128)(2,1)S(1)} %get-tuple-element.116.drel_ref, f32[400,2048]{1,0:T(8,128)S(1)} %relsum.7.refs_0_), custom_call_target="tpu_custom_call", output_to_operand_aliasing={{}: (2, {})} | custom-call | flops 838860800 | bytes 6553600 | tf_op jit(solution)/shard_map/relsum/pallas_call | solution.py:120
  113.3 2.2 %relsum.9.acc_ref = f32[400,2048]{1,0:T(8,128)S(1)} custom-call(s32[6,4,128]{2,1,0:T(4,128)S(1)} %copy-done.3, bf16[400,512]{1,0:T(8,128)(2,1)S(1)} %get-tuple-element.115.drel_ref, f32[400,2048]{1,0:T(8,128)S(1)} %relsum.8.refs_0_), custom_call_target="tpu_custom_call", output_to_operand_aliasing={{}: (2, {})} | custom-call | flops 838860800 | bytes 6553600 | tf_op jit(solution)/shard_map/relsum/pallas_call | solution.py:120
  115.8 2.2 %collective-permute-done.27.refs_3_ = bf16[400,128]{1,0:T(8,128)(2,1)S(1)} collective-permute-done((bf16[400,128]{1,0:T(8,128)(2,1)S(1)}, bf16[400,128]{1,0:T(8,128)(2,1)S(1)}, u32[]{:S(2)}, u32[]{:S(2)}) %collective-permute-start.27) | collective-permute-done | bytes 102432 | tf_op jit(solution)/shard_map/ppermute | solution.py:51
  118.0 3.0 %edges.11 = (f32[400,128]{1,0:T(8,128)S(1)}, bf16[400,128]{1,0:T(8,128)(2,1)S(1)}, bf16[400,128]{1,0:T(8,128)(2,1)S(1)}, bf16[400,128]{1,0:T(8,128)(2,1)S(1)}, bf16[400,512]{1,0:T(8,128)(2,1)S(1)}) custom-call(s32[2]{0:T(128)S(1)} %pad_add_fusion.me_ref, s32[6,4,128]{2,1,0:T(4,128)S(1)} %copy-done.9, s32[6,4,128]{2,1,0:T(4,128)S(1)} %copy-done.10, ...), custom_call_target="tpu_custom_call" | custom-call | flops 419430400 | bytes 2457600 | tf_op jit(solution)/shard_map/edges/pallas_call | solution.py:226
  121.0 2.0 %pieces.1 = (bf16[400,128]{1,0:T(8,128)(2,1)S(1)}, bf16[400,128]{1,0:T(8,128)(2,1)S(1)}, bf16[400,128]{1,0:T(8,128)(2,1)S(1)}, bf16[400,128]{1,0:T(8,128)(2,1)S(...) custom-call(s32[2]{0:T(128)S(1)} %pad_add_fusion.me_ref, ...), custom_call_target="tpu_custom_call" | custom-call | flops 838860800 | bytes 6553600 | tf_op jit(solution)/shard_map/pieces/pallas_call | solution.py:294
  126.7 4.2 %collective-permute-start.42 = (bf16[400,128]{1,0:T(8,128)(2,1)S(1)}, bf16[400,128]{1,0:T(8,128)(2,1)S(1)}, u32[]{:S(2)}, u32[]{:S(2)}) collective-permute-start(bf16[400,128]{1,0:T(8,128)(2,1)S(1)} %get-tuple-element.138), channel_id=1, source_target_pairs={{0,4},{2,6},{4,8},{6,10},{8,12},{10,14},{12,0},{14,2},{1,5},{3,7},... | collective-permute-start | bytes 307208 | tf_op jit(solution)/shard_map/ppermute | solution.py:41
  130.9 1.1 collective-permute-start.43
  132.0 2.3 %collective-permute-start.45 = (bf16[400,128]{1,0:T(8,128)(2,1)S(1)}, bf16[400,128]{1,0:T(8,128)(2,1)S(1)}, u32[]{:S(2)}, u32[]{:S(2)}) collective-permute-start(bf16[400,128]{1,0:T(8,128)(2,1)S(1)} %get-tuple-element.141), channel_id=1, source_target_pairs={{0,10},{2,12},{4,14},{6,0},{8,2},{10,4},{12,6},{14,8},{1,11},{3,13... | collective-permute-start | bytes 307208 | tf_op jit(solution)/shard_map/ppermute | solution.py:41
  134.3 2.4 %collective-permute-start.46 = (bf16[400,128]{1,0:T(8,128)(2,1)S(1)}, bf16[400,128]{1,0:T(8,128)(2,1)S(1)}, u32[]{:S(2)}, u32[]{:S(2)}) collective-permute-start(bf16[400,128]{1,0:T(8,128)(2,1)S(1)} %get-tuple-element.142), channel_id=1, source_target_pairs={{0,12},{2,14},{4,0},{6,2},{8,4},{10,6},{12,8},{14,10},{1,13},{3,15... | collective-permute-start | bytes 307208 | tf_op jit(solution)/shard_map/ppermute | solution.py:41
  137.0 6.6 %collective-permute-done.43.refs_3_ = bf16[400,128]{1,0:T(8,128)(2,1)S(1)} collective-permute-done((bf16[400,128]{1,0:T(8,128)(2,1)S(1)}, bf16[400,128]{1,0:T(8,128)(2,1)S(1)}, u32[]{:S(2)}, u32[]{:S(2)}) %collective-permute-start.43) | collective-permute-done | bytes 102432 | tf_op jit(solution)/shard_map/ppermute | solution.py:41
  143.6 2.4 %collective-permute-start.28 = (bf16[400,128]{1,0:T(8,128)(2,1)S(1)}, bf16[400,128]{1,0:T(8,128)(2,1)S(1)}, u32[]{:S(2)}, u32[]{:S(2)}) collective-permute-start(bf16[400,128]{1,0:T(8,128)(2,1)S(1)} %get-tuple-element.109), channel_id=1, source_target_pairs={{0,1},{1,0},{2,3},{3,2},{4,5},{5,4},{6,7},{7,6},{8,9},{9,8},{10,11... | collective-permute-start | bytes 307208 | tf_op jit(solution)/shard_map/ppermute | solution.py:45
  146.7 4.2 %collective-permute-start.30 = (bf16[400,128]{1,0:T(8,128)(2,1)S(1)}, bf16[400,128]{1,0:T(8,128)(2,1)S(1)}, u32[]{:S(2)}, u32[]{:S(2)}) collective-permute-start(bf16[400,128]{1,0:T(8,128)(2,1)S(1)} %get-tuple-element.111), channel_id=1, source_target_pairs={{0,11},{1,10},{2,13},{3,12},{4,15},{5,14},{6,1},{7,0},{8,3},{9,2},... | collective-permute-start | bytes 307208 | tf_op jit(solution)/shard_map/ppermute | solution.py:51
  151.0 3.9 %collective-permute-start.48 = (bf16[400,128]{1,0:T(8,128)(2,1)S(1)}, bf16[400,128]{1,0:T(8,128)(2,1)S(1)}, u32[]{:S(2)}, u32[]{:S(2)}) collective-permute-start(bf16[400,128]{1,0:T(8,128)(2,1)S(1)} %sum_all.1.refs_0_), channel_id=1, source_target_pairs={{0,2},{2,4},{4,6},{6,8},{8,10},{10,12},{12,14},{14,0},{1,3},{3,5},... | collective-permute-start | bytes 307208 | tf_op jit(solution)/shard_map/ppermute | solution.py:41
  155.5 1.4 update.11
  156.9 4.9 %collective-permute-start.50 = (bf16[400,128]{1,0:T(8,128)(2,1)S(1)}, bf16[400,128]{1,0:T(8,128)(2,1)}, u32[]{:S(2)}, u32[]{:S(2)}) collective-permute-start(bf16[400,128]{1,0:T(8,128)(2,1)S(1)} %sum_all.1.refs_0_), channel_id=1, source_target_pairs={{0,6},{2,8},{4,10},{6,12},{8,14},{10,0},{12,2},{14,4},{1,7},{3,9},... | collective-permute-start | bytes 307208 | tf_op jit(solution)/shard_map/ppermute | solution.py:41
  161.9 2.3 %collective-permute-start.51 = (bf16[400,128]{1,0:T(8,128)(2,1)S(1)}, bf16[400,128]{1,0:T(8,128)(2,1)}, u32[]{:S(2)}, u32[]{:S(2)}) collective-permute-start(bf16[400,128]{1,0:T(8,128)(2,1)S(1)} %sum_all.1.refs_0_), channel_id=1, source_target_pairs={{0,8},{2,10},{4,12},{6,14},{8,0},{10,2},{12,4},{14,6},{1,9},{3,11}... | collective-permute-start | bytes 307208 | tf_op jit(solution)/shard_map/ppermute | solution.py:41
  164.2 2.3 %collective-permute-start.52 = (bf16[400,128]{1,0:T(8,128)(2,1)S(1)}, bf16[400,128]{1,0:T(8,128)(2,1)}, u32[]{:S(2)}, u32[]{:S(2)}) collective-permute-start(bf16[400,128]{1,0:T(8,128)(2,1)S(1)} %sum_all.1.refs_0_), channel_id=1, source_target_pairs={{0,10},{2,12},{4,14},{6,0},{8,2},{10,4},{12,6},{14,8},{1,11},{3,13... | collective-permute-start | bytes 307208 | tf_op jit(solution)/shard_map/ppermute | solution.py:41
  166.5 1.9 %collective-permute-start.53 = (bf16[400,128]{1,0:T(8,128)(2,1)S(1)}, bf16[400,128]{1,0:T(8,128)(2,1)}, u32[]{:S(2)}, u32[]{:S(2)}) collective-permute-start(bf16[400,128]{1,0:T(8,128)(2,1)S(1)} %sum_all.1.refs_0_), channel_id=1, source_target_pairs={{0,12},{2,14},{4,0},{6,2},{8,4},{10,6},{12,8},{14,10},{1,13},{3,15... | collective-permute-start | bytes 307208 | tf_op jit(solution)/shard_map/ppermute | solution.py:41
  169.1 1.2 collective-permute-start.31
  170.3 5.2 %collective-permute-done.51.refs_4_ = bf16[400,128]{1,0:T(8,128)(2,1)} collective-permute-done((bf16[400,128]{1,0:T(8,128)(2,1)S(1)}, bf16[400,128]{1,0:T(8,128)(2,1)}, u32[]{:S(2)}, u32[]{:S(2)}) %collective-permute-start.51) | collective-permute-done | bytes 102432 | tf_op jit(solution)/shard_map/ppermute | solution.py:41
  177.5 4.2 %collective-permute-done.54.refs_7_ = bf16[400,128]{1,0:T(8,128)(2,1)S(1)} collective-permute-done((bf16[400,128]{1,0:T(8,128)(2,1)S(1)}, bf16[400,128]{1,0:T(8,128)(2,1)S(1)}, u32[]{:S(2)}, u32[]{:S(2)}) %collective-permute-start.54) | collective-permute-done | bytes 102432 | tf_op jit(solution)/shard_map/ppermute | solution.py:41
  183.4 2.0 %maximum_select_fusion = f32[400,256]{1,0:T(8,128)} fusion(f32[400,128]{1,0:T(8,128)} %collective-permute-done.31, f32[400,128]{1,0:T(8,128)} %get-tuple-element.112, pred[]{:T(512)S(6)} %eq.3), kind=kLoop, calls=%fused_computation | loop fusion | flops 307200 | bytes 819201 | tf_op jit(solution)/shard_map/jit(_where)/select_n | solution.py:423
  185.4 0.9 copy-done.6
  186.3 4.0 %relnew.1 = (f32[400,2048]{1,0:T(8,128)}, f32[1,2048]{1,0:T(1,128)}) custom-call(s32[2]{0:T(128)S(1)} %pad_add_fusion.me_ref, f32[400,2048]{1,0:T(8,128)S(1)} %copy-done.1, f32[1,2048]{1,0:T(1,128)S(1)} %bitcast.7, bf16[400,128]{1,0:T(8,128)(2,1)S(1)} %sum_all.1.refs_0_, bf16[400,128]{1,0:T(8,128)(2,1)S(1)} %collective-permute-done.48.refs_1_, ...), custom_call_target="tpu_custom_call" | custom-call | tf_op jit(solution)/shard_map/relnew/pallas_call | solution.py:357
  (116 shorter events, 22.1 us)
Async XLA Ops:
  10.3 1.7 collective-permute-start
  12.7 4.2 %collective-permute-start.1 = (bf16[400,128]{1,0:T(8,128)(2,1)S(1)}, bf16[400,128]{1,0:T(8,128)(2,1)S(1)}, u32[]{:S(2)}, u32[]{:S(2)}) collective-permute-start(bf16[400,128]{1,0:T(8,128)(2,1)S(1)} %get-tuple-element.79.refs_0_), channel_id=1, source_target_pairs={{0,1},{1,0},{2,3},{3,2},{4,5},{5,4},{6,7},{7,6},{8,9},{9,8},{10,11... | collective-permute-start | bytes 307208 | tf_op jit(solution)/shard_map/ppermute | solution.py:45
  13.1 5.2 %collective-permute-start.2 = (bf16[400,128]{1,0:T(8,128)(2,1)S(1)}, bf16[400,128]{1,0:T(8,128)(2,1)S(1)}, u32[]{:S(2)}, u32[]{:S(2)}) collective-permute-start(bf16[400,128]{1,0:T(8,128)(2,1)S(1)} %get-tuple-element.79.refs_0_), channel_id=1, source_target_pairs={{0,14},{2,0},{4,2},{6,4},{8,6},{10,8},{12,10},{14,12},{1,15},{3,1}... | collective-permute-start | bytes 307208 | tf_op jit(solution)/shard_map/ppermute | solution.py:41
  13.3 7.5 %collective-permute-start.3 = (bf16[400,128]{1,0:T(8,128)(2,1)S(1)}, bf16[400,128]{1,0:T(8,128)(2,1)S(1)}, u32[]{:S(2)}, u32[]{:S(2)}) collective-permute-start(bf16[400,128]{1,0:T(8,128)(2,1)S(1)} %get-tuple-element.79.refs_0_), channel_id=1, source_target_pairs={{0,15},{1,14},{2,1},{3,0},{4,3},{5,2},{6,5},{7,4},{8,7},{9,6},{10,... | collective-permute-start | bytes 307208 | tf_op jit(solution)/shard_map/ppermute | solution.py:51
  23.8 3.2 %collective-permute-start.4 = (bf16[400,128]{1,0:T(8,128)(2,1)S(1)}, bf16[400,128]{1,0:T(8,128)(2,1)S(1)}, u32[]{:S(2)}, u32[]{:S(2)}) collective-permute-start(bf16[400,128]{1,0:T(8,128)(2,1)S(1)} %get-tuple-element.81), channel_id=1, source_target_pairs={{0,1},{1,0},{2,3},{3,2},{4,5},{5,4},{6,7},{7,6},{8,9},{9,8},{10,11... | collective-permute-start | bytes 307208 | tf_op jit(solution)/shard_map/ppermute | solution.py:45
  24.0 4.1 %collective-permute-start.5 = (bf16[400,128]{1,0:T(8,128)(2,1)S(1)}, bf16[400,128]{1,0:T(8,128)(2,1)S(1)}, u32[]{:S(2)}, u32[]{:S(2)}) collective-permute-start(bf16[400,128]{1,0:T(8,128)(2,1)S(1)} %get-tuple-element.82), channel_id=1, source_target_pairs={{0,2},{2,4},{4,6},{6,8},{8,10},{10,12},{12,14},{14,0},{1,3},{3,5},... | collective-permute-start | bytes 307208 | tf_op jit(solution)/shard_map/ppermute | solution.py:41
  24.4 6.4 %collective-permute-start.6 = (bf16[400,128]{1,0:T(8,128)(2,1)S(1)}, bf16[400,128]{1,0:T(8,128)(2,1)S(1)}, u32[]{:S(2)}, u32[]{:S(2)}) collective-permute-start(bf16[400,128]{1,0:T(8,128)(2,1)S(1)} %get-tuple-element.83), channel_id=1, source_target_pairs={{0,3},{1,2},{2,5},{3,4},{4,7},{5,6},{6,9},{7,8},{8,11},{9,10},{10,... | collective-permute-start | bytes 307208 | tf_op jit(solution)/shard_map/ppermute | solution.py:51
  31.5 8.2 %collective-permute-start.7 = (bf16[400,128]{1,0:T(8,128)(2,1)S(1)}, bf16[400,128]{1,0:T(8,128)(2,1)S(1)}, u32[]{:S(2)}, u32[]{:S(2)}) collective-permute-start(bf16[400,128]{1,0:T(8,128)(2,1)S(1)} %get-tuple-element.86.refs_0_), channel_id=1, source_target_pairs={{0,1},{1,0},{2,3},{3,2},{4,5},{5,4},{6,7},{7,6},{8,9},{9,8},{10,11... | collective-permute-start | bytes 307208 | tf_op jit(solution)/shard_map/ppermute | solution.py:45
  31.5 8.1 %collective-permute-start.8 = (bf16[400,128]{1,0:T(8,128)(2,1)S(1)}, bf16[400,128]{1,0:T(8,128)(2,1)S(1)}, u32[]{:S(2)}, u32[]{:S(2)}) collective-permute-start(bf16[400,128]{1,0:T(8,128)(2,1)S(1)} %get-tuple-element.86.refs_0_), channel_id=1, source_target_pairs={{0,12},{2,14},{4,0},{6,2},{8,4},{10,6},{12,8},{14,10},{1,13},{3,15... | collective-permute-start | bytes 307208 | tf_op jit(solution)/shard_map/ppermute | solution.py:41
  32.7 7.5 %collective-permute-start.9 = (bf16[400,128]{1,0:T(8,128)(2,1)S(1)}, bf16[400,128]{1,0:T(8,128)(2,1)S(1)}, u32[]{:S(2)}, u32[]{:S(2)}) collective-permute-start(bf16[400,128]{1,0:T(8,128)(2,1)S(1)} %get-tuple-element.86.refs_0_), channel_id=1, source_target_pairs={{0,13},{1,12},{2,15},{3,14},{4,1},{5,0},{6,3},{7,2},{8,5},{9,4},{1... | collective-permute-start | bytes 307208 | tf_op jit(solution)/shard_map/ppermute | solution.py:51
  43.2 5.2 %collective-permute-start.10 = (bf16[400,128]{1,0:T(8,128)(2,1)S(1)}, bf16[400,128]{1,0:T(8,128)(2,1)S(1)}, u32[]{:S(2)}, u32[]{:S(2)}) collective-permute-start(bf16[400,128]{1,0:T(8,128)(2,1)S(1)} %get-tuple-element.88), channel_id=1, source_target_pairs={{0,1},{1,0},{2,3},{3,2},{4,5},{5,4},{6,7},{7,6},{8,9},{9,8},{10,11... | collective-permute-start | bytes 307208 | tf_op jit(solution)/shard_map/ppermute | solution.py:45
  43.6 5.4 %collective-permute-start.11 = (bf16[400,128]{1,0:T(8,128)(2,1)S(1)}, bf16[400,128]{1,0:T(8,128)(2,1)S(1)}, u32[]{:S(2)}, u32[]{:S(2)}) collective-permute-start(bf16[400,128]{1,0:T(8,128)(2,1)S(1)} %get-tuple-element.89), channel_id=1, source_target_pairs={{0,4},{2,6},{4,8},{6,10},{8,12},{10,14},{12,0},{14,2},{1,5},{3,7},... | collective-permute-start | bytes 307208 | tf_op jit(solution)/shard_map/ppermute | solution.py:41
  44.5 6.7 %collective-permute-start.12 = (bf16[400,128]{1,0:T(8,128)(2,1)S(1)}, bf16[400,128]{1,0:T(8,128)(2,1)S(1)}, u32[]{:S(2)}, u32[]{:S(2)}) collective-permute-start(bf16[400,128]{1,0:T(8,128)(2,1)S(1)} %get-tuple-element.90), channel_id=1, source_target_pairs={{0,5},{1,4},{2,7},{3,6},{4,9},{5,8},{6,11},{7,10},{8,13},{9,12},{1... | collective-permute-start | bytes 307208 | tf_op jit(solution)/shard_map/ppermute | solution.py:51
  51.9 7.0 %collective-permute-start.13 = (bf16[400,128]{1,0:T(8,128)(2,1)S(1)}, bf16[400,128]{1,0:T(8,128)(2,1)S(1)}, u32[]{:S(2)}, u32[]{:S(2)}) collective-permute-start(bf16[400,128]{1,0:T(8,128)(2,1)S(1)} %get-tuple-element.93.refs_0_), channel_id=1, source_target_pairs={{0,1},{1,0},{2,3},{3,2},{4,5},{5,4},{6,7},{7,6},{8,9},{9,8},{10,11... | collective-permute-start | bytes 307208 | tf_op jit(solution)/shard_map/ppermute | solution.py:45
  52.3 6.7 %collective-permute-start.14 = (bf16[400,128]{1,0:T(8,128)(2,1)S(1)}, bf16[400,128]{1,0:T(8,128)(2,1)S(1)}, u32[]{:S(2)}, u32[]{:S(2)}) collective-permute-start(bf16[400,128]{1,0:T(8,128)(2,1)S(1)} %get-tuple-element.93.refs_0_), channel_id=1, source_target_pairs={{0,10},{2,12},{4,14},{6,0},{8,2},{10,4},{12,6},{14,8},{1,11},{3,13... | collective-permute-start | bytes 307208 | tf_op jit(solution)/shard_map/ppermute | solution.py:41
  56.0 7.3 %collective-permute-start.15 = (bf16[400,128]{1,0:T(8,128)(2,1)S(1)}, bf16[400,128]{1,0:T(8,128)(2,1)S(1)}, u32[]{:S(2)}, u32[]{:S(2)}) collective-permute-start(bf16[400,128]{1,0:T(8,128)(2,1)S(1)} %get-tuple-element.93.refs_0_), channel_id=1, source_target_pairs={{0,11},{1,10},{2,13},{3,12},{4,15},{5,14},{6,1},{7,0},{8,3},{9,2},... | collective-permute-start | bytes 307208 | tf_op jit(solution)/shard_map/ppermute | solution.py:51
  66.3 9.9 %collective-permute-start.16 = (bf16[400,128]{1,0:T(8,128)(2,1)S(1)}, bf16[400,128]{1,0:T(8,128)(2,1)S(1)}, u32[]{:S(2)}, u32[]{:S(2)}) collective-permute-start(bf16[400,128]{1,0:T(8,128)(2,1)S(1)} %get-tuple-element.95), channel_id=1, source_target_pairs={{0,1},{1,0},{2,3},{3,2},{4,5},{5,4},{6,7},{7,6},{8,9},{9,8},{10,11... | collective-permute-start | bytes 307208 | tf_op jit(solution)/shard_map/ppermute | solution.py:45
  66.9 9.3 %collective-permute-start.17 = (bf16[400,128]{1,0:T(8,128)(2,1)S(1)}, bf16[400,128]{1,0:T(8,128)(2,1)S(1)}, u32[]{:S(2)}, u32[]{:S(2)}) collective-permute-start(bf16[400,128]{1,0:T(8,128)(2,1)S(1)} %get-tuple-element.96), channel_id=1, source_target_pairs={{0,6},{2,8},{4,10},{6,12},{8,14},{10,0},{12,2},{14,4},{1,7},{3,9},... | collective-permute-start | bytes 307208 | tf_op jit(solution)/shard_map/ppermute | solution.py:41
  68.8 10.0 %collective-permute-start.18 = (bf16[400,128]{1,0:T(8,128)(2,1)S(1)}, bf16[400,128]{1,0:T(8,128)(2,1)S(1)}, u32[]{:S(2)}, u32[]{:S(2)}) collective-permute-start(bf16[400,128]{1,0:T(8,128)(2,1)S(1)} %get-tuple-element.97), channel_id=1, source_target_pairs={{0,7},{1,6},{2,9},{3,8},{4,11},{5,10},{6,13},{7,12},{8,15},{9,14},... | collective-permute-start | bytes 307208 | tf_op jit(solution)/shard_map/ppermute | solution.py:51
  79.5 7.2 %collective-permute-start.19 = (bf16[400,128]{1,0:T(8,128)(2,1)S(1)}, bf16[400,128]{1,0:T(8,128)(2,1)S(1)}, u32[]{:S(2)}, u32[]{:S(2)}) collective-permute-start(bf16[400,128]{1,0:T(8,128)(2,1)S(1)} %get-tuple-element.100.refs_0_), channel_id=1, source_target_pairs={{0,1},{1,0},{2,3},{3,2},{4,5},{5,4},{6,7},{7,6},{8,9},{9,8},{10,11... | collective-permute-start | bytes 307208 | tf_op jit(solution)/shard_map/ppermute | solution.py:45
  80.0 6.7 %collective-permute-start.20 = (bf16[400,128]{1,0:T(8,128)(2,1)S(1)}, bf16[400,128]{1,0:T(8,128)(2,1)S(1)}, u32[]{:S(2)}, u32[]{:S(2)}) collective-permute-start(bf16[400,128]{1,0:T(8,128)(2,1)S(1)} %get-tuple-element.100.refs_0_), channel_id=1, source_target_pairs={{0,8},{2,10},{4,12},{6,14},{8,0},{10,2},{12,4},{14,6},{1,9},{3,11}... | collective-permute-start | bytes 307208 | tf_op jit(solution)/shard_map/ppermute | solution.py:41
  80.1 8.5 %collective-permute-start.21 = (bf16[400,128]{1,0:T(8,128)(2,1)S(1)}, bf16[400,128]{1,0:T(8,128)(2,1)S(1)}, u32[]{:S(2)}, u32[]{:S(2)}) collective-permute-start(bf16[400,128]{1,0:T(8,128)(2,1)S(1)} %get-tuple-element.100.refs_0_), channel_id=1, source_target_pairs={{0,9},{1,8},{2,11},{3,10},{4,13},{5,12},{6,15},{7,14},{8,1},{9,0},... | collective-permute-start | bytes 307208 | tf_op jit(solution)/shard_map/ppermute | solution.py:51
  91.6 8.5 %collective-permute-start.22 = (bf16[400,128]{1,0:T(8,128)(2,1)S(1)}, bf16[400,128]{1,0:T(8,128)(2,1)S(1)}, u32[]{:S(2)}, u32[]{:S(2)}) collective-permute-start(bf16[400,128]{1,0:T(8,128)(2,1)S(1)} %get-tuple-element.102), channel_id=1, source_target_pairs={{0,1},{1,0},{2,3},{3,2},{4,5},{5,4},{6,7},{7,6},{8,9},{9,8},{10,11... | collective-permute-start | bytes 307208 | tf_op jit(solution)/shard_map/ppermute | solution.py:45
  92.9 7.2 %collective-permute-start.23 = (bf16[400,128]{1,0:T(8,128)(2,1)S(1)}, bf16[400,128]{1,0:T(8,128)(2,1)S(1)}, u32[]{:S(2)}, u32[]{:S(2)}) collective-permute-start(bf16[400,128]{1,0:T(8,128)(2,1)S(1)} %get-tuple-element.103), channel_id=1, source_target_pairs={{0,8},{2,10},{4,12},{6,14},{8,0},{10,2},{12,4},{14,6},{1,9},{3,11}... | collective-permute-start | bytes 307208 | tf_op jit(solution)/shard_map/ppermute | solution.py:41
  95.3 8.4 %collective-permute-start.24 = (bf16[400,128]{1,0:T(8,128)(2,1)S(1)}, bf16[400,128]{1,0:T(8,128)(2,1)S(1)}, u32[]{:S(2)}, u32[]{:S(2)}) collective-permute-start(bf16[400,128]{1,0:T(8,128)(2,1)S(1)} %get-tuple-element.104), channel_id=1, source_target_pairs={{0,9},{1,8},{2,11},{3,10},{4,13},{5,12},{6,15},{7,14},{8,1},{9,0},... | collective-permute-start | bytes 307208 | tf_op jit(solution)/shard_map/ppermute | solution.py:51
  104.4 11.1 %collective-permute-start.25 = (bf16[400,128]{1,0:T(8,128)(2,1)S(1)}, bf16[400,128]{1,0:T(8,128)(2,1)S(1)}, u32[]{:S(2)}, u32[]{:S(2)}) collective-permute-start(bf16[400,128]{1,0:T(8,128)(2,1)S(1)} %get-tuple-element.107.refs_0_), channel_id=1, source_target_pairs={{0,1},{1,0},{2,3},{3,2},{4,5},{5,4},{6,7},{7,6},{8,9},{9,8},{10,11... | collective-permute-start | bytes 307208 | tf_op jit(solution)/shard_map/ppermute | solution.py:45
  105.7 10.1 %collective-permute-start.26 = (bf16[400,128]{1,0:T(8,128)(2,1)S(1)}, bf16[400,128]{1,0:T(8,128)(2,1)S(1)}, u32[]{:S(2)}, u32[]{:S(2)}) collective-permute-start(bf16[400,128]{1,0:T(8,128)(2,1)S(1)} %get-tuple-element.107.refs_0_), channel_id=1, source_target_pairs={{0,6},{2,8},{4,10},{6,12},{8,14},{10,0},{12,2},{14,4},{1,7},{3,9},... | collective-permute-start | bytes 307208 | tf_op jit(solution)/shard_map/ppermute | solution.py:41
  109.8 8.2 %collective-permute-start.27 = (bf16[400,128]{1,0:T(8,128)(2,1)S(1)}, bf16[400,128]{1,0:T(8,128)(2,1)S(1)}, u32[]{:S(2)}, u32[]{:S(2)}) collective-permute-start(bf16[400,128]{1,0:T(8,128)(2,1)S(1)} %get-tuple-element.107.refs_0_), channel_id=1, source_target_pairs={{0,7},{1,6},{2,9},{3,8},{4,11},{5,10},{6,13},{7,12},{8,15},{9,14},... | collective-permute-start | bytes 307208 | tf_op jit(solution)/shard_map/ppermute | solution.py:51
  121.0 64.4 %copy-start.7 = (f32[2048]{0:T(1024)S(1)}, f32[2048]{0:T(1024)}, u32[]{:S(2)}) copy-start(f32[2048]{0:T(1024)} %param.12) | copy-start | bytes 24580
  123.1 1.6 collective-permute-start.33
  123.6 1.3 collective-permute-start.34
  123.7 1.5 collective-permute-start.35
  124.1 1.3 collective-permute-start.36
  124.2 1.4 collective-permute-start.37
  124.6 1.3 collective-permute-start.38
  124.9 1.3 collective-permute-start.39
  125.1 1.3 collective-permute-start.40
  126.6 7.6 %collective-permute-start.41 = (bf16[400,128]{1,0:T(8,128)(2,1)S(1)}, bf16[400,128]{1,0:T(8,128)(2,1)S(1)}, u32[]{:S(2)}, u32[]{:S(2)}) collective-permute-start(bf16[400,128]{1,0:T(8,128)(2,1)S(1)} %get-tuple-element.137), channel_id=1, source_target_pairs={{0,2},{2,4},{4,6},{6,8},{8,10},{10,12},{12,14},{14,0},{1,3},{3,5},... | collective-permute-start | bytes 307208 | tf_op jit(solution)/shard_map/ppermute | solution.py:41
  126.7 9.9 %collective-permute-start.42 = (bf16[400,128]{1,0:T(8,128)(2,1)S(1)}, bf16[400,128]{1,0:T(8,128)(2,1)S(1)}, u32[]{:S(2)}, u32[]{:S(2)}) collective-permute-start(bf16[400,128]{1,0:T(8,128)(2,1)S(1)} %get-tuple-element.138), channel_id=1, source_target_pairs={{0,4},{2,6},{4,8},{6,10},{8,12},{10,14},{12,0},{14,2},{1,5},{3,7},... | collective-permute-start | bytes 307208 | tf_op jit(solution)/shard_map/ppermute | solution.py:41
  130.9 12.7 %collective-permute-start.43 = (bf16[400,128]{1,0:T(8,128)(2,1)S(1)}, bf16[400,128]{1,0:T(8,128)(2,1)S(1)}, u32[]{:S(2)}, u32[]{:S(2)}) collective-permute-start(bf16[400,128]{1,0:T(8,128)(2,1)S(1)} %get-tuple-element.139), channel_id=1, source_target_pairs={{0,6},{2,8},{4,10},{6,12},{8,14},{10,0},{12,2},{14,4},{1,7},{3,9},... | collective-permute-start | bytes 307208 | tf_op jit(solution)/shard_map/ppermute | solution.py:41
  132.0 14.0 %collective-permute-start.44 = (bf16[400,128]{1,0:T(8,128)(2,1)S(1)}, bf16[400,128]{1,0:T(8,128)(2,1)S(1)}, u32[]{:S(2)}, u32[]{:S(2)}) collective-permute-start(bf16[400,128]{1,0:T(8,128)(2,1)S(1)} %get-tuple-element.140), channel_id=1, source_target_pairs={{0,8},{2,10},{4,12},{6,14},{8,0},{10,2},{12,4},{14,6},{1,9},{3,11}... | collective-permute-start | bytes 307208 | tf_op jit(solution)/shard_map/ppermute | solution.py:41
  132.0 14.7 %collective-permute-start.45 = (bf16[400,128]{1,0:T(8,128)(2,1)S(1)}, bf16[400,128]{1,0:T(8,128)(2,1)S(1)}, u32[]{:S(2)}, u32[]{:S(2)}) collective-permute-start(bf16[400,128]{1,0:T(8,128)(2,1)S(1)} %get-tuple-element.141), channel_id=1, source_target_pairs={{0,10},{2,12},{4,14},{6,0},{8,2},{10,4},{12,6},{14,8},{1,11},{3,13... | collective-permute-start | bytes 307208 | tf_op jit(solution)/shard_map/ppermute | solution.py:41
  134.3 16.6 %collective-permute-start.46 = (bf16[400,128]{1,0:T(8,128)(2,1)S(1)}, bf16[400,128]{1,0:T(8,128)(2,1)S(1)}, u32[]{:S(2)}, u32[]{:S(2)}) collective-permute-start(bf16[400,128]{1,0:T(8,128)(2,1)S(1)} %get-tuple-element.142), channel_id=1, source_target_pairs={{0,12},{2,14},{4,0},{6,2},{8,4},{10,6},{12,8},{14,10},{1,13},{3,15... | collective-permute-start | bytes 307208 | tf_op jit(solution)/shard_map/ppermute | solution.py:41
  136.6 14.3 %collective-permute-start.47 = (bf16[400,128]{1,0:T(8,128)(2,1)S(1)}, bf16[400,128]{1,0:T(8,128)(2,1)S(1)}, u32[]{:S(2)}, u32[]{:S(2)}) collective-permute-start(bf16[400,128]{1,0:T(8,128)(2,1)S(1)} %get-tuple-element.143), channel_id=1, source_target_pairs={{0,14},{2,0},{4,2},{6,4},{8,6},{10,8},{12,10},{14,12},{1,15},{3,1}... | collective-permute-start | bytes 307208 | tf_op jit(solution)/shard_map/ppermute | solution.py:41
  143.6 11.4 %collective-permute-start.28 = (bf16[400,128]{1,0:T(8,128)(2,1)S(1)}, bf16[400,128]{1,0:T(8,128)(2,1)S(1)}, u32[]{:S(2)}, u32[]{:S(2)}) collective-permute-start(bf16[400,128]{1,0:T(8,128)(2,1)S(1)} %get-tuple-element.109), channel_id=1, source_target_pairs={{0,1},{1,0},{2,3},{3,2},{4,5},{5,4},{6,7},{7,6},{8,9},{9,8},{10,11... | collective-permute-start | bytes 307208 | tf_op jit(solution)/shard_map/ppermute | solution.py:45
  146.0 9.0 %collective-permute-start.29 = (bf16[400,128]{1,0:T(8,128)(2,1)S(1)}, bf16[400,128]{1,0:T(8,128)(2,1)S(1)}, u32[]{:S(2)}, u32[]{:S(2)}) collective-permute-start(bf16[400,128]{1,0:T(8,128)(2,1)S(1)} %get-tuple-element.110), channel_id=1, source_target_pairs={{0,10},{2,12},{4,14},{6,0},{8,2},{10,4},{12,6},{14,8},{1,11},{3,13... | collective-permute-start | bytes 307208 | tf_op jit(solution)/shard_map/ppermute | solution.py:41
  146.7 8.8 %collective-permute-start.30 = (bf16[400,128]{1,0:T(8,128)(2,1)S(1)}, bf16[400,128]{1,0:T(8,128)(2,1)S(1)}, u32[]{:S(2)}, u32[]{:S(2)}) collective-permute-start(bf16[400,128]{1,0:T(8,128)(2,1)S(1)} %get-tuple-element.111), channel_id=1, source_target_pairs={{0,11},{1,10},{2,13},{3,12},{4,15},{5,14},{6,1},{7,0},{8,3},{9,2},... | collective-permute-start | bytes 307208 | tf_op jit(solution)/shard_map/ppermute | solution.py:51
  151.0 15.5 %collective-permute-start.48 = (bf16[400,128]{1,0:T(8,128)(2,1)S(1)}, bf16[400,128]{1,0:T(8,128)(2,1)S(1)}, u32[]{:S(2)}, u32[]{:S(2)}) collective-permute-start(bf16[400,128]{1,0:T(8,128)(2,1)S(1)} %sum_all.1.refs_0_), channel_id=1, source_target_pairs={{0,2},{2,4},{4,6},{6,8},{8,10},{10,12},{12,14},{14,0},{1,3},{3,5},... | collective-permute-start | bytes 307208 | tf_op jit(solution)/shard_map/ppermute | solution.py:41
  155.0 13.5 %collective-permute-start.49 = (bf16[400,128]{1,0:T(8,128)(2,1)S(1)}, bf16[400,128]{1,0:T(8,128)(2,1)S(1)}, u32[]{:S(2)}, u32[]{:S(2)}) collective-permute-start(bf16[400,128]{1,0:T(8,128)(2,1)S(1)} %sum_all.1.refs_0_), channel_id=1, source_target_pairs={{0,4},{2,6},{4,8},{6,10},{8,12},{10,14},{12,0},{14,2},{1,5},{3,7},... | collective-permute-start | bytes 307208 | tf_op jit(solution)/shard_map/ppermute | solution.py:41
  156.9 7.3 %collective-permute-start.32 = (f32[1,128]{1,0:T(1,128)S(1)}, f32[1,128]{1,0:T(1,128)S(1)}, u32[]{:S(2)}, u32[]{:S(2)}) collective-permute-start(f32[1,128]{1,0:T(1,128)S(1)} %get-tuple-element.113), channel_id=1, source_target_pairs={{0,1},{1,0},{2,3},{3,2},{4,5},{5,4},{6,7},{7,6},{8,9},{9,8},{10,11... | collective-permute-start | bytes 1544 | tf_op jit(solution)/shard_map/ppermute | solution.py:45
  156.9 13.4 %collective-permute-start.50 = (bf16[400,128]{1,0:T(8,128)(2,1)S(1)}, bf16[400,128]{1,0:T(8,128)(2,1)}, u32[]{:S(2)}, u32[]{:S(2)}) collective-permute-start(bf16[400,128]{1,0:T(8,128)(2,1)S(1)} %sum_all.1.refs_0_), channel_id=1, source_target_pairs={{0,6},{2,8},{4,10},{6,12},{8,14},{10,0},{12,2},{14,4},{1,7},{3,9},... | collective-permute-start | bytes 307208 | tf_op jit(solution)/shard_map/ppermute | solution.py:41
  161.9 13.7 %collective-permute-start.51 = (bf16[400,128]{1,0:T(8,128)(2,1)S(1)}, bf16[400,128]{1,0:T(8,128)(2,1)}, u32[]{:S(2)}, u32[]{:S(2)}) collective-permute-start(bf16[400,128]{1,0:T(8,128)(2,1)S(1)} %sum_all.1.refs_0_), channel_id=1, source_target_pairs={{0,8},{2,10},{4,12},{6,14},{8,0},{10,2},{12,4},{14,6},{1,9},{3,11}... | collective-permute-start | bytes 307208 | tf_op jit(solution)/shard_map/ppermute | solution.py:41
  164.2 11.7 %collective-permute-start.52 = (bf16[400,128]{1,0:T(8,128)(2,1)S(1)}, bf16[400,128]{1,0:T(8,128)(2,1)}, u32[]{:S(2)}, u32[]{:S(2)}) collective-permute-start(bf16[400,128]{1,0:T(8,128)(2,1)S(1)} %sum_all.1.refs_0_), channel_id=1, source_target_pairs={{0,10},{2,12},{4,14},{6,0},{8,2},{10,4},{12,6},{14,8},{1,11},{3,13... | collective-permute-start | bytes 307208 | tf_op jit(solution)/shard_map/ppermute | solution.py:41
  166.5 10.0 %collective-permute-start.53 = (bf16[400,128]{1,0:T(8,128)(2,1)S(1)}, bf16[400,128]{1,0:T(8,128)(2,1)}, u32[]{:S(2)}, u32[]{:S(2)}) collective-permute-start(bf16[400,128]{1,0:T(8,128)(2,1)S(1)} %sum_all.1.refs_0_), channel_id=1, source_target_pairs={{0,12},{2,14},{4,0},{6,2},{8,4},{10,6},{12,8},{14,10},{1,13},{3,15... | collective-permute-start | bytes 307208 | tf_op jit(solution)/shard_map/ppermute | solution.py:41
  169.1 13.2 %collective-permute-start.31 = (f32[400,128]{1,0:T(8,128)}, f32[400,128]{1,0:T(8,128)}, u32[]{:S(2)}, u32[]{:S(2)}) collective-permute-start(f32[400,128]{1,0:T(8,128)} %get-tuple-element.112), channel_id=1, source_target_pairs={{0,1},{1,0},{2,3},{3,2},{4,5},{5,4},{6,7},{7,6},{8,9},{9,8},{10,11... | collective-permute-start | bytes 614408 | tf_op jit(solution)/shard_map/ppermute | solution.py:45
  170.3 11.4 %collective-permute-start.54 = (bf16[400,128]{1,0:T(8,128)(2,1)S(1)}, bf16[400,128]{1,0:T(8,128)(2,1)S(1)}, u32[]{:S(2)}, u32[]{:S(2)}) collective-permute-start(bf16[400,128]{1,0:T(8,128)(2,1)S(1)} %sum_all.1.refs_0_), channel_id=1, source_target_pairs={{0,14},{2,0},{4,2},{6,4},{8,6},{10,8},{12,10},{14,12},{1,15},{3,1}... | collective-permute-start | bytes 307208 | tf_op jit(solution)/shard_map/ppermute | solution.py:41
  175.5 6.8 %collective-permute-start.55 = (bf16[400,128]{1,0:T(8,128)(2,1)S(1)}, bf16[400,128]{1,0:T(8,128)(2,1)S(1)}, u32[]{:S(2)}, u32[]{:S(2)}) collective-permute-start(bf16[400,128]{1,0:T(8,128)(2,1)S(1)} %sum_all.1.refs_0_), channel_id=1, source_target_pairs={{0,1},{1,0},{2,3},{3,2},{4,5},{5,4},{6,7},{7,6},{8,9},{9,8},{10,11... | collective-permute-start | bytes 307208 | tf_op jit(solution)/shard_map/ppermute | solution.py:45
  175.9 6.9 %collective-permute-start.56 = (bf16[400,128]{1,0:T(8,128)(2,1)S(1)}, bf16[400,128]{1,0:T(8,128)(2,1)S(1)}, u32[]{:S(2)}, u32[]{:S(2)}) collective-permute-start(bf16[400,128]{1,0:T(8,128)(2,1)S(1)} %collective-permute-done.48.refs_1_), channel_id=1, source_target_pairs={{0,1},{1,0},{2,3},{3,2},{4,5},{5,4},{6,7},{7,6},{8,9},{9,8},{10,11... | collective-permute-start | bytes 307208 | tf_op jit(solution)/shard_map/ppermute | solution.py:45
  176.5 6.4 %collective-permute-start.57 = (bf16[400,128]{1,0:T(8,128)(2,1)}, bf16[400,128]{1,0:T(8,128)(2,1)S(1)}, u32[]{:S(2)}, u32[]{:S(2)}) collective-permute-start(bf16[400,128]{1,0:T(8,128)(2,1)} %copy-done.5), channel_id=1, source_target_pairs={{0,1},{1,0},{2,3},{3,2},{4,5},{5,4},{6,7},{7,6},{8,9},{9,8},{10,11... | collective-permute-start | bytes 307208 | tf_op jit(solution)/shard_map/ppermute | solution.py:45
  181.7 3.7 %collective-permute-start.58 = (bf16[400,128]{1,0:T(8,128)(2,1)}, bf16[400,128]{1,0:T(8,128)(2,1)S(1)}, u32[]{:S(2)}, u32[]{:S(2)}) collective-permute-start(bf16[400,128]{1,0:T(8,128)(2,1)} %collective-permute-done.50.refs_3_), channel_id=1, source_target_pairs={{0,1},{1,0},{2,3},{3,2},{4,5},{5,4},{6,7},{7,6},{8,9},{9,8},{10,11... | collective-permute-start | bytes 307208 | tf_op jit(solution)/shard_map/ppermute | solution.py:45
  182.3 3.1 %collective-permute-start.59 = (bf16[400,128]{1,0:T(8,128)(2,1)}, bf16[400,128]{1,0:T(8,128)(2,1)S(1)}, u32[]{:S(2)}, u32[]{:S(2)}) collective-permute-start(bf16[400,128]{1,0:T(8,128)(2,1)} %collective-permute-done.51.refs_4_), channel_id=1, source_target_pairs={{0,1},{1,0},{2,3},{3,2},{4,5},{5,4},{6,7},{7,6},{8,9},{9,8},{10,11... | collective-permute-start | bytes 307208 | tf_op jit(solution)/shard_map/ppermute | solution.py:45
  182.3 3.1 %collective-permute-start.60 = (bf16[400,128]{1,0:T(8,128)(2,1)}, bf16[400,128]{1,0:T(8,128)(2,1)S(1)}, u32[]{:S(2)}, u32[]{:S(2)}) collective-permute-start(bf16[400,128]{1,0:T(8,128)(2,1)} %collective-permute-done.52.refs_5_), channel_id=1, source_target_pairs={{0,1},{1,0},{2,3},{3,2},{4,5},{5,4},{6,7},{7,6},{8,9},{9,8},{10,11... | collective-permute-start | bytes 307208 | tf_op jit(solution)/shard_map/ppermute | solution.py:45
  182.8 2.6 %collective-permute-start.61 = (bf16[400,128]{1,0:T(8,128)(2,1)}, bf16[400,128]{1,0:T(8,128)(2,1)S(1)}, u32[]{:S(2)}, u32[]{:S(2)}) collective-permute-start(bf16[400,128]{1,0:T(8,128)(2,1)} %collective-permute-done.53.refs_6_), channel_id=1, source_target_pairs={{0,1},{1,0},{2,3},{3,2},{4,5},{5,4},{6,7},{7,6},{8,9},{9,8},{10,11... | collective-permute-start | bytes 307208 | tf_op jit(solution)/shard_map/ppermute | solution.py:45
  182.9 2.5 %collective-permute-start.62 = (bf16[400,128]{1,0:T(8,128)(2,1)S(1)}, bf16[400,128]{1,0:T(8,128)(2,1)S(1)}, u32[]{:S(2)}, u32[]{:S(2)}) collective-permute-start(bf16[400,128]{1,0:T(8,128)(2,1)S(1)} %collective-permute-done.54.refs_7_), channel_id=1, source_target_pairs={{0,1},{1,0},{2,3},{3,2},{4,5},{5,4},{6,7},{7,6},{8,9},{9,8},{10,11... | collective-permute-start | bytes 307208 | tf_op jit(solution)/shard_map/ppermute | solution.py:45
  (10 other events, 50.2 us)
